TPU v7x, 32 devices: a whole 2x2x4 slice. The times are simulated.
32 devices in a mesh: dp: 8 (over z, x), row: 2 (over y), col: 2 (over core).
Axes of the slice: x: 2, y: 2, z: 4, core: 2. Of those that a mesh axis runs over, the one named last changes fastest.
Arguments:
- tokens: bfloat16 [32768, 640], P('dp', ('row', 'col')), may hold values from -6 to 6
- w_query: bfloat16 [640, 1024], P('row', 'col'), may hold values from -0.25 to 0.25
- w_key: bfloat16 [640, 256], P('row', 'col'), may hold values from -0.25 to 0.25
- w_value: bfloat16 [640, 256], P('row', 'col'), may hold values from -0.25 to 0.25
- w_out: bfloat16 [1024, 640], P('col', 'row'), may hold values from -0.1875 to 0.1875
- w_gate: bfloat16 [640, 2048], P('row', 'col'), may hold values from -0.25 to 0.25
- w_up: bfloat16 [640, 2048], P('row', 'col'), may hold values from -0.25 to 0.25
- w_down: bfloat16 [2048, 640], P('col', 'row'), may hold values from -0.125 to 0.125
- gain_input: float32 [640], P(('row', 'col')), may hold values from 0.1 to 1.9
- gain_post_attn: float32 [640], P(('row', 'col')), may hold values from 0.1 to 1.9
- gain_pre_ffn: float32 [640], P(('row', 'col')), may hold values from 0.1 to 1.9
- gain_post_ffn: float32 [640], P(('row', 'col')), may hold values from 0.1 to 1.9
- gain_query: float32 [256], replicated, may hold values from 0.1 to 1.9
- gain_key: float32 [256], replicated, may hold values from 0.1 to 1.9
- segment_ids: int32 [32768], P('dp'), may hold values from 0 to 127, never falling along the last dimension, each value on 1 to 512 neighbouring positions
- positions: int32 [32768], P('dp'), may hold values from 0 to 8191
- cotangent: bfloat16 [32768, 640], P('dp', ('row', 'col')), may hold values from -6 to 6
Outputs:
- output: bfloat16 [32768, 640], P('dp', ('row', 'col'))
- grad_tokens: bfloat16 [32768, 640], P('dp', ('row', 'col'))
- grad_w_query: float32 [640, 1024], P('row', 'col')
- grad_w_key: float32 [640, 256], P('row', 'col')
- grad_w_value: float32 [640, 256], P('row', 'col')
- grad_w_out: float32 [1024, 640], P('col', 'row')
- grad_w_gate: float32 [640, 2048], P('row', 'col')
- grad_w_up: float32 [640, 2048], P('row', 'col')
- grad_w_down: float32 [2048, 640], P('col', 'row')
- grad_gain_input: float32 [640], P(('row', 'col'))
- grad_gain_post_attn: float32 [640], P(('row', 'col'))
- grad_gain_pre_ffn: float32 [640], P(('row', 'col'))
- grad_gain_post_ffn: float32 [640], P(('row', 'col'))
- grad_gain_query: float32 [256], replicated
- grad_gain_key: float32 [256], replicated
Inputs may be any that keep to these rules, and one draw needn't show every extreme that they name: segment_ids never fall from one token to the next; each document has 1 to min(512, 1024) tokens.
All inputs are finite; a program needn't handle non-finite values.
Results may differ from a plain program's by a relative error of at most 0.02.
Values may be sent and summed in bfloat16 or wider, within the bound.
A program may use at most 192 MiB of HBM per device.

v0:
```python
import math

import jax
import jax.numpy as jnp
from jax import lax
from jax.sharding import PartitionSpec as P

D = 640
HD = 256
LEN = 1024


EPSILON = 1e-06
ROPE_BASE = 1000000.0
MASK_VALUE = -1000000000.0


def shortened(array):
    return jax.tree.map(lambda a: a.astype(jnp.bfloat16) if a.dtype == jnp.float32 else a, array)


def contract_rows(left, right):
    return lax.dot_general(
        left, right, (((0,), (0,)), ((), ())), preferred_element_type=jnp.float32
    )


def contract_cols(left, right):
    return lax.dot_general(
        left, right, (((1,), (1,)), ((), ())), preferred_element_type=jnp.float32
    )


def feature_sum(values):
    return lax.psum(values, ("row", "col"))


def gather_features(values):
    return lax.all_gather(values, "col", axis=1, tiled=True)


def sum_hidden(values):
    return lax.psum_scatter(values, "row", scatter_dimension=1, tiled=True)


def gather_hidden(values):
    return jax.tree.map(
        lambda part, own: part.astype(own.dtype),
        lax.all_gather(shortened(values), "row", axis=1, tiled=True),
        values,
    )


def sum_features(values):
    return lax.psum_scatter(values, "col", scatter_dimension=1, tiled=True)


def total_gains(values):
    return lax.psum(values, ("dp", "row", "col"))


def norm_apply(values, gain_vec, summer):
    totals = summer(jnp.sum(values * values, axis=1))
    inv_rms = lax.rsqrt(totals / D + EPSILON)
    return (values * inv_rms[:, None] * gain_vec[None, :], inv_rms)


def norm_back(values, inv_rms, gain_vec, grad_out, summer):
    weighted = grad_out * gain_vec[None, :]
    row_inner = summer(jnp.sum(weighted * values, axis=1))
    grad_in = inv_rms[:, None] * weighted - values * (inv_rms**3 * row_inner / D)[:, None]
    grad_gain = jnp.sum(grad_out * values * inv_rms[:, None], axis=0)
    return (grad_in, grad_gain)


def rotary_tables(positions, width):
    half_width = width // 2
    frequency = jnp.exp(
        jnp.arange(half_width, dtype=jnp.float32) * (-2.0 * math.log(ROPE_BASE) / width)
    )
    angles = positions.astype(jnp.float32)[:, None] * frequency[None, :]
    return (jnp.cos(angles), jnp.sin(angles))


def head_prep(values, gain_vec, cosine, sine):
    inv_rms = lax.rsqrt(jnp.mean(values * values, axis=-1, keepdims=True) + EPSILON)
    normed = values * inv_rms * gain_vec
    half_width = normed.shape[-1] // 2
    first_half = normed[..., :half_width]
    second = normed[..., half_width:]
    return jnp.concatenate(
        [first_half * cosine - second * sine, second * cosine + first_half * sine], axis=-1
    )


def masked_scores(query_seq, key_seq, seg_seq):
    width = query_seq.shape[0]
    causal = jnp.arange(width)[:, None] >= jnp.arange(width)[None, :]
    allowed = causal & (seg_seq[:, None] == seg_seq[None, :])
    scale_factor = query_seq.shape[-1] ** (-0.5)
    scores = (
        jnp.einsum("qd,kd->qk", query_seq, key_seq, preferred_element_type=jnp.float32)
        * scale_factor
    )
    return (jnp.where(allowed, scores, MASK_VALUE), scale_factor)


def attend(inputs):
    query_seq, key_seq, value_seq, seg_seq = inputs
    scores, scale_factor = masked_scores(query_seq, key_seq, seg_seq)
    row_max = jnp.max(scores, axis=1)
    exp_scores = jnp.exp(scores - row_max[:, None])
    row_total = jnp.sum(exp_scores, axis=1)
    soft_weights = (exp_scores / row_total[:, None]).astype(jnp.bfloat16)
    return (
        jnp.dot(soft_weights, value_seq, preferred_element_type=jnp.float32),
        row_max,
        row_total,
    )


def attend_back(inputs):
    query_seq, key_seq, value_seq, seg_seq, row_max, row_total, grad_seq = inputs
    scores, scale_factor = masked_scores(query_seq, key_seq, seg_seq)
    soft_weights = jnp.exp(scores - row_max[:, None]) / row_total[:, None]
    grad_weights = jnp.einsum("qd,kd->qk", grad_seq, value_seq, preferred_element_type=jnp.float32)
    row_inner = jnp.sum(grad_weights * soft_weights, axis=1)
    grad_scores = (soft_weights * (grad_weights - row_inner[:, None])).astype(jnp.bfloat16)
    grad_query = jnp.dot(grad_scores, key_seq, preferred_element_type=jnp.float32) * scale_factor
    grad_key = (
        jnp.einsum("qk,qd->kd", grad_scores, query_seq, preferred_element_type=jnp.float32)
        * scale_factor
    )
    grad_value = jnp.einsum(
        "qk,qd->kd", soft_weights.astype(jnp.bfloat16), grad_seq, preferred_element_type=jnp.float32
    )
    return (grad_query, grad_key, grad_value)


def gelu_product(gate_act, up_act):
    return jax.nn.gelu(gate_act, approximate=True) * up_act


def grid_block(
    tokens,
    w_query,
    w_key,
    w_value,
    w_out,
    w_gate,
    w_up,
    w_down,
    gain_input,
    gain_post_attn,
    gain_pre_ffn,
    gain_post_ffn,
    gain_query,
    gain_key,
    segment_ids,
    positions,
    cotangent,
):
    residual = tokens.astype(jnp.float32)
    row_count = residual.shape[0]
    seq_count = row_count // LEN
    col_index = lax.axis_index("col")
    key_width = w_key.shape[1]
    normed_in, inv_in = norm_apply(residual, gain_input, feature_sum)
    act_one = gather_features(normed_in.astype(jnp.bfloat16))
    query_raw = sum_hidden(jnp.dot(act_one, w_query, preferred_element_type=jnp.float32))
    key_part = jnp.dot(act_one, w_key, preferred_element_type=jnp.float32)
    value_part = jnp.dot(act_one, w_value, preferred_element_type=jnp.float32)
    key_sum, value_sum = lax.psum((key_part, value_part), "row")
    key_raw, value_full = (
        lax.all_gather(key_sum, "col", axis=1, tiled=True),
        lax.all_gather(value_sum, "col", axis=1, tiled=True),
    )
    cosine, sine = rotary_tables(positions, HD)
    query_head = head_prep(query_raw, gain_query, cosine, sine).astype(jnp.bfloat16)
    key_head = head_prep(key_raw, gain_key, cosine, sine).astype(jnp.bfloat16)
    value_head = value_full.astype(jnp.bfloat16)
    query_seqs = query_head.reshape(seq_count, LEN, HD)
    key_seqs = key_head.reshape(seq_count, LEN, HD)
    value_seqs = value_head.reshape(seq_count, LEN, HD)
    seg_seqs = segment_ids.reshape(seq_count, LEN)
    heads_out, row_maxes, row_totals = lax.map(attend, (query_seqs, key_seqs, value_seqs, seg_seqs))
    attn_head = heads_out.reshape(row_count, HD).astype(jnp.bfloat16)
    attn_gathered = gather_hidden(attn_head)
    branch_attn = sum_features(jnp.dot(attn_gathered, w_out, preferred_element_type=jnp.float32))
    post_attn, inv_attn = norm_apply(branch_attn, gain_post_attn, feature_sum)
    middle = residual + post_attn
    normed_ffn, inv_pre = norm_apply(middle, gain_pre_ffn, feature_sum)
    act_two = gather_features(normed_ffn.astype(jnp.bfloat16))
    gate_act, up_act = sum_hidden(
        (
            jnp.dot(act_two, w_gate, preferred_element_type=jnp.float32),
            jnp.dot(act_two, w_up, preferred_element_type=jnp.float32),
        )
    )
    hidden = gelu_product(gate_act, up_act).astype(jnp.bfloat16)
    hidden_gathered = gather_hidden(hidden)
    branch_ffn = sum_features(jnp.dot(hidden_gathered, w_down, preferred_element_type=jnp.float32))
    post_ffn, inv_ffn = norm_apply(branch_ffn, gain_post_ffn, feature_sum)
    result = (middle + post_ffn).astype(jnp.bfloat16)
    grad_result = cotangent.astype(jnp.float32)
    grad_branch_ffn, grad_gain_post_ffn = norm_back(
        branch_ffn, inv_ffn, gain_post_ffn, grad_result, feature_sum
    )
    grad_ffn_out = gather_features(grad_branch_ffn.astype(jnp.bfloat16))
    grad_w_down = contract_rows(hidden_gathered, grad_ffn_out)
    grad_hidden = sum_hidden(contract_cols(grad_ffn_out, w_down))
    unused_value, pull_gelu = jax.vjp(gelu_product, gate_act, up_act)
    grad_gate, grad_up = pull_gelu(grad_hidden)
    grad_gate_all, grad_up_all = gather_hidden(
        (grad_gate.astype(jnp.bfloat16), grad_up.astype(jnp.bfloat16))
    )
    grad_w_gate = contract_rows(act_two, grad_gate_all)
    grad_w_up = contract_rows(act_two, grad_up_all)
    grad_act_two = sum_features(
        contract_cols(grad_gate_all, w_gate) + contract_cols(grad_up_all, w_up)
    )
    grad_pre_norm, grad_gain_pre_ffn = norm_back(
        middle, inv_pre, gain_pre_ffn, grad_act_two, feature_sum
    )
    grad_middle = grad_result + grad_pre_norm
    grad_branch_attn, grad_gain_post_attn = norm_back(
        branch_attn, inv_attn, gain_post_attn, grad_middle, feature_sum
    )
    grad_attn_out = gather_features(grad_branch_attn.astype(jnp.bfloat16))
    grad_w_out = contract_rows(attn_gathered, grad_attn_out)
    grad_head = sum_hidden(contract_cols(grad_attn_out, w_out)).astype(jnp.bfloat16)
    grad_query_seq, grad_key_seq, grad_value_seq = lax.map(
        attend_back,
        (
            query_seqs,
            key_seqs,
            value_seqs,
            seg_seqs,
            row_maxes,
            row_totals,
            grad_head.reshape(seq_count, LEN, HD),
        ),
    )
    grad_key_rot, grad_value = (
        lax.psum(grad_key_seq.reshape(row_count, HD).astype(jnp.bfloat16), ("row", "col")).astype(
            jnp.float32
        ),
        lax.psum(grad_value_seq.reshape(row_count, HD).astype(jnp.bfloat16), ("row", "col")).astype(
            jnp.float32
        ),
    )

    def prep_one(values, gain_vec):
        return head_prep(values, gain_vec, cosine, sine)

    unused_query, pull_query = jax.vjp(prep_one, query_raw, gain_query)
    grad_query_raw, grad_gain_query = pull_query(grad_query_seq.reshape(row_count, HD))
    unused_key, pull_key = jax.vjp(prep_one, key_raw, gain_key)
    grad_key_raw, grad_gain_key = pull_key(grad_key_rot)
    grad_gain_query = total_gains(grad_gain_query)
    grad_query_all = gather_hidden(grad_query_raw.astype(jnp.bfloat16))
    grad_key_block = lax.dynamic_slice_in_dim(
        grad_key_raw.astype(jnp.bfloat16), col_index * key_width, key_width, 1
    )
    grad_value_block = lax.dynamic_slice_in_dim(
        grad_value.astype(jnp.bfloat16), col_index * key_width, key_width, 1
    )
    grad_w_query = contract_rows(act_one, grad_query_all)
    grad_w_key = contract_rows(act_one, grad_key_block)
    grad_w_value = contract_rows(act_one, grad_value_block)
    grad_act_one = sum_features(
        contract_cols(grad_query_all, w_query)
        + contract_cols(grad_key_block, w_key)
        + contract_cols(grad_value_block, w_value)
    )
    grad_in_norm, grad_gain_input = norm_back(
        residual, inv_in, gain_input, grad_act_one, feature_sum
    )
    grad_tokens = (grad_middle + grad_in_norm).astype(jnp.bfloat16)
    (
        grad_w_query,
        grad_w_key,
        grad_w_value,
        grad_w_out,
        grad_w_gate,
        grad_w_up,
        grad_w_down,
        grad_gain_input,
        grad_gain_post_attn,
        grad_gain_pre_ffn,
        grad_gain_post_ffn,
        grad_gain_key,
    ) = lax.psum(
        (
            grad_w_query,
            grad_w_key,
            grad_w_value,
            grad_w_out,
            grad_w_gate,
            grad_w_up,
            grad_w_down,
            grad_gain_input,
            grad_gain_post_attn,
            grad_gain_pre_ffn,
            grad_gain_post_ffn,
            grad_gain_key,
        ),
        "dp",
    )
    return (
        result,
        grad_tokens,
        grad_w_query,
        grad_w_key,
        grad_w_value,
        grad_w_out,
        grad_w_gate,
        grad_w_up,
        grad_w_down,
        grad_gain_input,
        grad_gain_post_attn,
        grad_gain_pre_ffn,
        grad_gain_post_ffn,
        grad_gain_query,
        grad_gain_key,
    )


def local(
    tokens,
    w_query,
    w_key,
    w_value,
    w_out,
    w_gate,
    w_up,
    w_down,
    gain_input,
    gain_post_attn,
    gain_pre_ffn,
    gain_post_ffn,
    gain_query,
    gain_key,
    segment_ids,
    positions,
    cotangent,
):
    return grid_block(
        tokens,
        w_query,
        w_key,
        w_value,
        w_out,
        w_gate,
        w_up,
        w_down,
        gain_input,
        gain_post_attn,
        gain_pre_ffn,
        gain_post_ffn,
        gain_query,
        gain_key,
        segment_ids,
        positions,
        cotangent,
    )


def solution(mesh):
    in_specs = (
        P("dp", ("row", "col")),
        P("row", "col"),
        P("row", "col"),
        P("row", "col"),
        P("col", "row"),
        P("row", "col"),
        P("row", "col"),
        P("col", "row"),
        P(("row", "col")),
        P(("row", "col")),
        P(("row", "col")),
        P(("row", "col")),
        P(),
        P(),
        P("dp"),
        P("dp"),
        P("dp", ("row", "col")),
    )
    out_specs = (
        P("dp", ("row", "col")),
        P("dp", ("row", "col")),
        P("row", "col"),
        P("row", "col"),
        P("row", "col"),
        P("col", "row"),
        P("row", "col"),
        P("row", "col"),
        P("col", "row"),
        P(("row", "col")),
        P(("row", "col")),
        P(("row", "col")),
        P(("row", "col")),
        P(),
        P(),
    )
    return jax.shard_map(local, mesh=mesh, in_specs=in_specs, out_specs=out_specs, check_vma=False)
```

profile of v0, /device:TPU:0, one launch (start us, length us, event | category | flops | bytes accessed | tf_op | source)
XLA Modules:
  0.0 2059.7 jit_solution(12070926243237755543)
XLA Ops:
  8.9 12.7 psum.175
  41.1 64.2 %all-reduce.12.cloned.1.call-done = f32[4096,128]{1,0:T(8,128)} async-done(((f32[4096,128]{1,0:T(8,128)}), f32[4096,128]{1,0:T(8,128)}) %all-reduce.12.cloned.1.call-update) | async-done | bytes 2097168 | tf_op jit(solution)/shard_map/psum | solution.py:173
  118.0 91.4 %all-reduce.17 = bf16[4096,128]{1,0:T(8,128)(2,1)} all-reduce(f32[4096,128]{1,0:T(8,128)} %fusion.120), channel_id=1, replica_groups=mesh['dp'=8,'row'=2,'col'=2] {'row'}, use_global_device_ids=true, to_apply=%region_6.0 | all-reduce | flops 524288 | bytes 3145728 | tf_op jit(solution)/shard_map/psum | solution.py:173
  216.3 43.2 %reduce-scatter.10.cloned.1.call-done = f32[4096,256]{1,0:T(8,128)} async-done(((f32[4096,512]{1,0:T(8,128)}), f32[4096,256]{1,0:T(8,128)}) %reduce-scatter.10.cloned.1.call-update) | async-done | bytes 4194320 | tf_op jit(solution)/shard_map/reduce_scatter | solution.py:43
  277.5 19.8 while.30
  298.8 56.8 %all-gather.18.cloned.1.call-done = bf16[4096,512]{1,0:T(8,128)(2,1)} async-done(((bf16[4096,256]{1,0:T(8,128)(2,1)}), bf16[4096,512]{1,0:T(8,128)(2,1)}) %all-gather.18.cloned.1.call-update) | async-done | bytes 4194320 | tf_op jit(solution)/shard_map/all_gather | solution.py:49
  361.8 13.3 reduce-scatter.12.cloned.1.call-done
  426.8 12.6 fusion.122
  439.5 177.8 %reduce-scatter.16.cloned.1.call-done = f32[4096,512]{1,0:T(8,128)} async-done(((f32[4096,1024]{1,0:T(8,128)}), f32[4096,512]{1,0:T(8,128)}) %reduce-scatter.16.cloned.1.call-update) | async-done | bytes 8388624 | tf_op jit(solution)/shard_map/reduce_scatter | solution.py:43
  617.3 191.3 %reduce-scatter.14.cloned.1.call-done = f32[4096,512]{1,0:T(8,128)} async-done(((f32[4096,1024]{1,0:T(8,128)}), f32[4096,512]{1,0:T(8,128)}) %reduce-scatter.14.cloned.1.call-update) | async-done | bytes 8388624 | tf_op jit(solution)/shard_map/reduce_scatter | solution.py:43
  817.7 103.7 %all-gather.22.cloned.1.call-done = bf16[4096,1024]{1,0:T(8,128)(2,1)} async-done(((bf16[4096,512]{1,0:T(8,128)(2,1)}), bf16[4096,1024]{1,0:T(8,128)(2,1)}) %all-gather.22.cloned.1.call-update) | async-done | bytes 8388624 | tf_op jit(solution)/shard_map/all_gather | solution.py:49
  932.3 13.3 reduce-scatter.18.cloned.1.call-done
  999.0 190.4 %reduce-scatter.20.cloned.1.call-done = f32[4096,512]{1,0:T(8,128)} async-done(((f32[4096,1024]{1,0:T(8,128)}), f32[4096,512]{1,0:T(8,128)}) %reduce-scatter.20.cloned.1.call-update) | async-done | bytes 8388624 | tf_op jit(solution)/shard_map/reduce_scatter | solution.py:43
  1189.4 14.8 multiply_convert_fusion.1
  1205.1 103.4 %all-gather.26.cloned.1.call-done = bf16[4096,1024]{1,0:T(8,128)(2,1)} async-done(((bf16[4096,512]{1,0:T(8,128)(2,1)}), bf16[4096,1024]{1,0:T(8,128)(2,1)}) %all-gather.26.cloned.1.call-update) | async-done | bytes 8388624 | tf_op jit(solution)/shard_map/all_gather | solution.py:49
  1319.2 94.7 %all-gather.28.cloned.1.call-done = bf16[4096,1024]{1,0:T(8,128)(2,1)} async-done(((bf16[4096,512]{1,0:T(8,128)(2,1)}), bf16[4096,1024]{1,0:T(8,128)(2,1)}) %all-gather.28.cloned.1.call-update) | async-done | bytes 8388624 | tf_op jit(solution)/shard_map/all_gather | solution.py:49
  1424.4 13.3 reduce-scatter.22.cloned.1.call-done
  1495.2 97.7 %reduce-scatter.24.cloned.1.call-done = f32[4096,256]{1,0:T(8,128)} async-done(((f32[4096,512]{1,0:T(8,128)}), f32[4096,256]{1,0:T(8,128)}) %reduce-scatter.24.cloned.1.call-update) | async-done | bytes 4194320 | tf_op jit(solution)/shard_map/reduce_scatter | solution.py:43
  1596.7 47.8 %while.31 = (s32[]{:T(128)}, f32[4,1024,256]{2,1,0:T(8,128)}, bf16[4,1024,256]{2,1,0:T(8,128)(2,1)S(1)}, bf16[4,1024,256]{2,1,0:T(8,128)(2,1)}, s32[4,1024]{1,0:...) while((s32[]{:T(128)}, f32[4,1024,256]{2,1,0:T(8,128)}, ...), condition=%wide.region_32.33_spmd.clone, body=%wide.region_30.32_spmd.sunk.clone | while | flops 2698509312 | bytes 63493328 | solution.py:232
  1645.9 85.8 %all-reduce.16.cloned.1.call-done = (bf16[4096,256]{1,0:T(8,128)(2,1)}, bf16[4096,256]{1,0:T(8,128)(2,1)}) async-done(((bf16[4096,256]{1,0:T(8,128)(2,1)}, bf16[4096,256]{1,0:T(8,128)(2,1)}), (bf16[4096,256]{1,0:T(8,128)(2,1)}, bf16[4096,256]{1,0:T(8,128)(2,1)})) %all-reduce.16.cloned.1.call-update) | async-done | bytes 4194320 | tf_op jit(solution)/shard_map/psum | solution.py:245
  1756.0 50.7 %all-gather.32.cloned.1.call-done = bf16[4096,512]{1,0:T(8,128)(2,1)} async-done(((bf16[4096,256]{1,0:T(8,128)(2,1)}), bf16[4096,512]{1,0:T(8,128)(2,1)}) %all-gather.32.cloned.1.call-update) | async-done | bytes 4194320 | tf_op jit(solution)/shard_map/all_gather | solution.py:49
  1845.1 45.5 %psum.198 = f32[256]{0:T(256)} all-reduce(f32[256]{0:T(256)S(1)} %get-tuple-element.124), channel_id=1, replica_groups=mesh['dp'=8,'row'=2,'col'=2] {'dp','row','col'}, use_global_device_ids=true, to_apply=%region_56.57 | all-reduce | flops 256 | bytes 2048 | tf_op jit(solution)/shard_map/psum | solution.py:59
  1893.2 22.9 %all-reduce.4 = (f32[160]{0:T(256)}, f32[160]{0:T(256)}, f32[160]{0:T(256)}, f32[160]{0:T(256)}, f32[256]{0:T(256)}) all-reduce(f32[160]{0:T(256)S(1)} %get-tuple-element.134, f32[160]{0:T(256)S(1)} %copy-done.62, f32[160]{0:T(256)S(1)} %copy-done.61, f32[160]{0:T(256)S(1)} %copy-done.60, ...), channel_id=1, replica_groups=mesh['dp'=8,'row'=2,'col'=2] {'dp'}, use_global_device_ids=true, to_apply=%region_48.49 | all-reduce | flops 896 | bytes 7168 | tf_op jit(solution)/shard_map/psum | solution.py:293
  1930.5 112.0 %all-reduce.14.cloned.1.call-done = (f32[320,512]{1,0:T(8,128)}, f32[320,128]{1,0:T(8,128)}, f32[320,128]{1,0:T(8,128)}, f32[512,320]{0,1:T(8,128)}, f32[320,102...) async-done(((f32[320,512]{1,0:T(8,128)}, f32[320,128]{1,0:T(8,128)}, f32[320,128]{1,0:T(8,128)}, f32[512,320]{0,1:T(8,128)}, f32[320,1024]{1,0:T(8,128)}, ...) | async-done | bytes 5570576 | tf_op jit(solution)/shard_map/psum | solution.py:293
  (348 shorter events, 432.8 us)
Async XLA Ops:
  7.2 914.2 %copy-start = (bf16[1024,320]{0,1:T(8,128)(2,1)S(1)}, bf16[1024,320]{0,1:T(8,128)(2,1)}, u32[]{:S(2)}) copy-start(bf16[1024,320]{0,1:T(8,128)(2,1)} %param.28) | copy-start | bytes 1966084
  7.2 29.6 %all-gather.12.cloned.1.call-start = ((), (), s32[]{:S(2)}) async-start(), calls=%async_computation.9 | async-start | bytes 3932160 | tf_op jit(solution)/shard_map/all_gather | solution.py:39
  25.0 80.3 %all-reduce.12.cloned.1.call-start = ((), (), s32[]{:S(2)}) async-start(), calls=%async_computation.11 | async-start | bytes 4194304 | tf_op jit(solution)/shard_map/psum | solution.py:173
  41.0 168.7 %all-gather.14.cloned.1.call-start = ((), (), s32[]{:S(2)}) async-start(), calls=%async_computation.12 | async-start | bytes 6291456 | tf_op jit(solution)/shard_map/all_gather | solution.py:175
  105.3 154.3 %reduce-scatter.10.cloned.1.call-start = ((), (), s32[]{:S(2)}) async-start(), calls=%async_computation.10 | async-start | bytes 12582912 | tf_op jit(solution)/shard_map/reduce_scatter | solution.py:43
  112.0 165.5 %all-gather.16.cloned.1.call-start = ((), (), s32[]{:S(2)}) async-start(), calls=%async_computation.13 | async-start | bytes 3145728 | tf_op jit(solution)/shard_map/all_gather | solution.py:176
  209.5 146.1 %all-gather.18.cloned.1.call-start = ((), (), s32[]{:S(2)}) async-start(), calls=%async_computation.14 | async-start | bytes 6291456 | tf_op jit(solution)/shard_map/all_gather | solution.py:49
  298.7 76.3 %reduce-scatter.12.cloned.1.call-start = ((), (), s32[]{:S(2)}) async-start(), calls=%async_computation.15 | async-start | bytes 7864320 | tf_op jit(solution)/shard_map/reduce_scatter | solution.py:55
  361.7 52.9 %all-gather.20.cloned.1.call-start = ((), (), s32[]{:S(2)}) async-start(), calls=%async_computation.16 | async-start | bytes 3932160 | tf_op jit(solution)/shard_map/all_gather | solution.py:39
  403.0 214.3 %reduce-scatter.16.cloned.1.call-start = ((), (), s32[]{:S(2)}) async-start(), calls=%async_computation.18 | async-start | bytes 25165824 | tf_op jit(solution)/shard_map/reduce_scatter | solution.py:43
  426.8 381.7 %reduce-scatter.14.cloned.1.call-start = ((), (), s32[]{:S(2)}) async-start(), calls=%async_computation.17 | async-start | bytes 25165824 | tf_op jit(solution)/shard_map/reduce_scatter | solution.py:43
  439.4 481.9 %all-gather.22.cloned.1.call-start = ((), (), s32[]{:S(2)}) async-start(), calls=%async_computation.19 | async-start | bytes 12582912 | tf_op jit(solution)/shard_map/all_gather | solution.py:49
  817.2 128.4 %reduce-scatter.18.cloned.1.call-start = ((), (), s32[]{:S(2)}) async-start(), calls=%async_computation.20 | async-start | bytes 7864320 | tf_op jit(solution)/shard_map/reduce_scatter | solution.py:55
  932.2 56.8 %all-gather.24.cloned.1.call-start = ((), (), s32[]{:S(2)}) async-start(), calls=%async_computation.21 | async-start | bytes 3932160 | tf_op jit(solution)/shard_map/all_gather | solution.py:39
  977.4 212.0 %reduce-scatter.20.cloned.1.call-start = ((), (), s32[]{:S(2)}) async-start(), calls=%async_computation.22 | async-start | bytes 25165824 | tf_op jit(solution)/shard_map/reduce_scatter | solution.py:43
  999.0 309.5 %all-gather.26.cloned.1.call-start = ((), (), s32[]{:S(2)}) async-start(), calls=%async_computation.23 | async-start | bytes 12582912 | tf_op jit(solution)/shard_map/all_gather | solution.py:49
  1204.3 209.7 %all-gather.28.cloned.1.call-start = ((), (), s32[]{:S(2)}) async-start(), calls=%async_computation.24 | async-start | bytes 12582912 | tf_op jit(solution)/shard_map/all_gather | solution.py:49
  1204.9 232.9 %reduce-scatter.22.cloned.1.call-start = ((), (), s32[]{:S(2)}) async-start(), calls=%async_computation.25 | async-start | bytes 7864320 | tf_op jit(solution)/shard_map/reduce_scatter | solution.py:55
  1424.4 60.6 %all-gather.30.cloned.1.call-start = ((), (), s32[]{:S(2)}) async-start(), calls=%async_computation.26 | async-start | bytes 3932160 | tf_op jit(solution)/shard_map/all_gather | solution.py:39
  1473.3 119.6 %reduce-scatter.24.cloned.1.call-start = ((), (), s32[]{:S(2)}) async-start(), calls=%async_computation.27 | async-start | bytes 12582912 | tf_op jit(solution)/shard_map/reduce_scatter | solution.py:43
  1492.4 239.3 %all-reduce.16.cloned.1.call-start = ((), (), s32[]{:S(2)}) async-start(), calls=%async_computation.31 | async-start | bytes 8388608 | tf_op jit(solution)/shard_map/psum | solution.py:245
  1645.9 160.8 %all-gather.32.cloned.1.call-start = ((), (), s32[]{:S(2)}) async-start(), calls=%async_computation.28 | async-start | bytes 6291456 | tf_op jit(solution)/shard_map/all_gather | solution.py:49
  1749.7 140.9 %reduce-scatter.26.cloned.1.call-start = ((), (), s32[]{:S(2)}) async-start(), calls=%async_computation.29 | async-start | bytes 7864320 | tf_op jit(solution)/shard_map/reduce_scatter | solution.py:55
  1815.4 227.2 %all-reduce.14.cloned.1.call-start = ((), (), s32[]{:S(2)}) async-start(), calls=%async_computation.30 | async-start | bytes 11141120 | tf_op jit(solution)/shard_map/psum | solution.py:293
  (77 other events, 1436.2 us)
Sparse Core Ops, SparseCore 0:
  25.1 11.6 all-gather.11
  41.1 64.0 all-reduce.11
  106.9 12.9 all-gather.13
  122.2 137.3 reduce-scatter.9
  261.5 10.3 all-gather.15
  298.9 56.7 all-gather.17
  361.8 13.1 reduce-scatter.11
  403.1 11.4 all-gather.19
  426.9 190.2 reduce-scatter.15
  619.4 189.0 reduce-scatter.13
  817.3 104.0 all-gather.21
  932.3 13.1 reduce-scatter.17
  977.5 11.4 all-gather.23
  999.1 190.2 reduce-scatter.19
  1204.4 104.0 all-gather.25
  1309.9 103.9 all-gather.27
  1424.5 13.1 reduce-scatter.21
  1473.5 11.4 all-gather.29
  1492.5 100.4 reduce-scatter.23
  1646.0 85.6 all-reduce.15
  1749.8 56.8 all-gather.31
  1815.5 13.1 reduce-scatter.25
  1845.2 197.2 all-reduce.13
where the time goes:
time: 2070 us; the launch traced here: 2060 us
  waiting for transfers between devices  1460 us (71%)
  blocking collectives  248 us (12%)
  matrix products  189 us (9%)
  other arithmetic  120 us (6%)
  local copies, waits for them, and re-layouts  26.3 us (1%)
    reduce_scatter x5, waiting for transfers between devices, sum_hidden(): return lax.psum_scatter(values, 'row', scatter_dimension=1, tiled=True)  700 us
    all_gather x5, waiting for transfers between devices, gather_hidden(): lax.all_gather(shortened(values), 'row', axis=1, tiled=True)  409 us
    psum x1, waiting for transfers between devices, grid_block(): lax.psum((grad_w_query, grad_w_key, grad_w_value, grad_w_out, grad_w_gate...  112 us
    psum x1, blocking collectives, grid_block(): key_sum, value_sum = lax.psum((key_part, value_part), 'row')  91.4 us
    psum x8, blocking collectives, feature_sum(): return lax.psum(values, ('row', 'col'))  88 us
    psum x1, waiting for transfers between devices, grid_block(): lax.psum(grad_key_seq.reshape(row_count, HD).astype(jnp.bfloat16), ('row'...  85.8 us
    psum x1, waiting for transfers between devices, grid_block(): key_sum, value_sum = lax.psum((key_part, value_part), 'row')  64.2 us
    dot_general x7, matrix products, contract_cols(): lax.dot_general(left, right, (((1,), (1,)), ((), ())), preferred_element_...  46.4 us
  transfers between devices with their start and end apart: 23, of which 20 were waited for; matrix products, arithmetic and copies ran while one was open for 5% of the time, Pallas kernels for 0%

commit v1 on v0

v1 whole, which is shorter than its diff:
```python
import math

import jax
import jax.numpy as jnp
from jax import lax
from jax.experimental import pallas as pl
from jax.experimental.pallas import tpu as pltpu
from jax.sharding import PartitionSpec as P

D = 640
HEADS = 4
HD = 256
FF = 2048
LEN = 1024

EPSILON = 1e-06
ROPE_BASE = 1000000.0
MASK_VALUE = -1000000000.0
GROUP = ("row", "col")
BF16 = jnp.bfloat16
F32 = jnp.float32
SCALE = HD ** -0.5


def dot(left, right):
    return jnp.dot(left, right, preferred_element_type=F32)


def dot_rows(left, right):
    return lax.dot_general(left, right, (((0,), (0,)), ((), ())), preferred_element_type=F32)


def dot_cols(left, right):
    return lax.dot_general(left, right, (((1,), (1,)), ((), ())), preferred_element_type=F32)


def inverse_rms(values):
    return lax.rsqrt(jnp.mean(values * values, axis=-1, keepdims=True) + EPSILON)


def norm_back(values, inv_rms, gain, grad):
    weighted = grad * gain
    inner = jnp.mean(weighted * values, axis=-1, keepdims=True)
    return inv_rms * weighted - values * (inv_rms * inv_rms * inv_rms * inner)


def gain_back(values, inv_rms, grad):
    return jnp.sum(grad * values * inv_rms, axis=0)


def rotary_tables(positions):
    half = HD // 2
    frequency = jnp.exp(jnp.arange(half, dtype=F32) * (-2.0 * math.log(ROPE_BASE) / HD))
    angles = positions.astype(F32)[:, None] * frequency[None, :]
    return (jnp.cos(angles), jnp.sin(angles))


def gather_blocks(block):
    rows, cols = lax.axis_size("row"), lax.axis_size("col")
    return lax.all_gather(block, GROUP).reshape(rows, cols, *block.shape)


def scatter_blocks(blocks):
    blocks = blocks.reshape(-1, *blocks.shape[2:])
    return lax.psum_scatter(blocks, GROUP, scatter_dimension=0)


def to_tokens(block):
    return lax.all_to_all(block, GROUP, split_axis=0, concat_axis=1, tiled=True)


def to_features(block):
    return lax.all_to_all(block, GROUP, split_axis=1, concat_axis=0, tiled=True)


BLOCK = 256
REACH = 512


def window(start):
    return max(0, start - REACH), start + BLOCK


def joined(ref):
    block = ref[:, 0]
    return block.reshape(block.shape[0] * block.shape[1], block.shape[2])


def joined_cols(ref):
    sides = [ref[:, c].reshape(-1, ref.shape[3]) for c in range(ref.shape[1])]
    return jnp.concatenate(sides, axis=1)


def prep(raw, gain, cosine, sine):
    normed = raw * inverse_rms(raw) * gain
    first, second = normed[:, : HD // 2], normed[:, HD // 2 :]
    return jnp.concatenate(
        [first * cosine - second * sine, second * cosine + first * sine], axis=1
    ).astype(BF16)


def prep_back(raw, gain, cosine, sine, grad):
    first, second = grad[:, : HD // 2], grad[:, HD // 2 :]
    turned = jnp.concatenate(
        [first * cosine + second * sine, second * cosine - first * sine], axis=1
    )
    inv = inverse_rms(raw)
    return norm_back(raw, inv, gain, turned).astype(BF16), gain_back(raw, inv, turned)


def attention_kernel(
    x_ref, wq_ref, wk_ref, wv_ref, wo_ref, g_in, g_attn, g_query, g_key, cos_ref, sin_ref, seg_col, seg_row,
    qraw_ref, kraw_ref, qh_ref, kh_ref, v_ref, attn_ref, yo_ref, middle_ref, a1_s,
):
    head = pl.program_id(1)
    cosine, sine = cos_ref[...], sin_ref[...]

    @pl.when(head == 0)
    def _():
        x = x_ref[...].astype(F32)
        a1 = (x * inverse_rms(x) * g_in[...]).astype(BF16)
        a1_s[...] = a1
        k_raw = dot(a1, joined_cols(wk_ref))
        kraw_ref[...] = k_raw
        kh_ref[...] = prep(k_raw, g_key[...], cosine, sine)
        v_ref[...] = dot(a1, joined_cols(wv_ref)).astype(BF16)
        yo_ref[...] = jnp.zeros_like(yo_ref)

    q_raw = dot(a1_s[...], joined(wq_ref))
    qraw_ref[...] = q_raw
    qh_ref[...] = prep(q_raw, g_query[...], cosine, sine)
    for start in range(0, LEN, BLOCK):
        low, high = window(start)
        rows = slice(start, high)
        scores = dot_cols(qh_ref[rows, :] * SCALE, kh_ref[low:high, :])
        place_q = start + lax.broadcasted_iota(jnp.int32, scores.shape, 0)
        place_k = low + lax.broadcasted_iota(jnp.int32, scores.shape, 1)
        allowed = (place_q >= place_k) & (seg_col[rows, :] == seg_row[0][:, low:high])
        scores = jnp.where(allowed, scores, MASK_VALUE)
        exps = jnp.exp(scores - jnp.max(scores, axis=1, keepdims=True))
        probs = (exps * (1.0 / jnp.sum(exps, axis=1, keepdims=True))).astype(BF16)
        attn_ref[rows, :] = dot(probs, v_ref[low:high, :]).astype(BF16)
    yo_ref[...] += dot_cols(attn_ref[...], joined(wo_ref))

    @pl.when(head == HEADS - 1)
    def _():
        y_o = yo_ref[...]
        middle_ref[...] = x_ref[...].astype(F32) + y_o * inverse_rms(y_o) * g_attn[...]


def attention_back_kernel(
    x_ref, wq_ref, wk_ref, wv_ref, wo_ref, g_in, g_attn, g_query, g_key, cos_ref, sin_ref, seg_col, seg_row,
    qraw_ref, kraw_ref, qh_ref, kh_ref, v_ref, attn_ref, yo_ref, dmid_ref,
    gw_q, gw_k, gw_v, gw_o, gx_ref, gg_in, gg_attn, gg_query, gg_key,
    a1_s, dyo_s, dq_s, dk_s, dv_s, da1_s, g_s,
):
    head = pl.program_id(1)
    cosine, sine = cos_ref[...], sin_ref[...]

    @pl.when(head == 0)
    def _():
        x = x_ref[...].astype(F32)
        a1_s[...] = (x * inverse_rms(x) * g_in[...]).astype(BF16)
        y_o, d_middle = yo_ref[...], dmid_ref[...]
        inv = inverse_rms(y_o)
        dyo_s[...] = norm_back(y_o, inv, g_attn[...], d_middle).astype(BF16)
        gg_attn[...] = gain_back(y_o, inv, d_middle)[None]
        dk_s[...] = jnp.zeros_like(dk_s)
        dv_s[...] = jnp.zeros_like(dv_s)
        da1_s[...] = jnp.zeros_like(da1_s)
        gg_query[...] = jnp.zeros_like(gg_query)

    d_yo, a1 = dyo_s[...], a1_s[...]
    gw_o[...] = dot_rows(d_yo, attn_ref[...]).astype(BF16).reshape(gw_o.shape)
    g_s[...] = dot(d_yo, joined(wo_ref)).astype(BF16)
    for start in range(0, LEN, BLOCK):
        low, high = window(start)
        rows = slice(start, high)
        query, grad = qh_ref[rows, :] * SCALE, g_s[rows, :]
        scores = dot_cols(kh_ref[low:high, :], query)
        place_k = low + lax.broadcasted_iota(jnp.int32, scores.shape, 0)
        place_q = start + lax.broadcasted_iota(jnp.int32, scores.shape, 1)
        allowed = (place_q >= place_k) & (seg_col[low:high, :] == seg_row[0][:, rows])
        scores = jnp.where(allowed, scores, MASK_VALUE)
        exps = jnp.exp(scores - jnp.max(scores, axis=0, keepdims=True))
        probs = exps * (1.0 / jnp.sum(exps, axis=0, keepdims=True))
        dp = dot_cols(v_ref[low:high, :], grad)
        ds = (probs * (dp - jnp.sum(dp * probs, axis=0, keepdims=True))).astype(BF16)
        dq_s[rows, :] = dot_rows(ds, kh_ref[low:high, :]) * SCALE
        dk_s[low:high, :] += dot(ds, query)
        dv_s[low:high, :] += dot(probs.astype(BF16), grad)
    d_q, gg = prep_back(qraw_ref[...], g_query[...], cosine, sine, dq_s[...])
    gg_query[...] += gg[None]
    gw_q[...] = dot_rows(a1, d_q).astype(BF16).reshape(gw_q.shape)
    da1_s[...] += dot_cols(d_q, joined(wq_ref))

    @pl.when(head == HEADS - 1)
    def _():
        d_k, gg = prep_back(kraw_ref[...], g_key[...], cosine, sine, dk_s[...])
        gg_key[...] = gg[None]
        d_v = dv_s[...].astype(BF16)
        for ref, grad in ((gw_k, d_k), (gw_v, d_v)):
            whole = dot_rows(a1, grad).astype(BF16)
            width = ref.shape[3]
            for c in range(ref.shape[1]):
                ref[:, c] = whole[:, c * width : (c + 1) * width].reshape(ref.shape[0], ref.shape[2], width)
        d_a1 = da1_s[...] + dot_cols(d_k, joined_cols(wk_ref)) + dot_cols(d_v, joined_cols(wv_ref))
        x = x_ref[...].astype(F32)
        inv = inverse_rms(x)
        gx_ref[...] = (dmid_ref[...] + norm_back(x, inv, g_in[...], d_a1)).astype(BF16)
        gg_in[...] = gain_back(x, inv, d_a1)[None]


def attention_specs(weights):
    rows, cols, depth, width = weights.shape
    per = HEADS // cols
    narrow = HD // cols
    wide = per * HD

    def token(width):
        return pl.BlockSpec((LEN, width), lambda s, h: (s, 0))

    def fixed(width):
        return pl.BlockSpec((1, width), lambda s, h: (0, 0))

    def heads(first):
        return pl.BlockSpec((rows, 1, depth, HD), lambda s, h: (0, h // per, 0, first + h % per))

    def share(which):
        return pl.BlockSpec((rows, cols, depth, narrow), lambda s, h: (0, 0, 0, which))

    base = wide // narrow
    in_specs = [
        token(D), heads(0), share(base), share(base + 1), heads((wide + 2 * narrow) // HD),
        fixed(D), fixed(D), fixed(HD), fixed(HD), token(HD // 2), token(HD // 2),
        token(1), pl.BlockSpec((1, 1, LEN), lambda s, h: (s, 0, 0)),
    ]
    head = pl.BlockSpec((LEN, HD), lambda s, h: (s, h))
    saved = [head, token(HD), head, token(HD), token(HD), head, token(D)]
    return in_specs, saved, token(D), heads, share, fixed


def attention_inputs(x, weights, gains, cosine, sine, segs):
    return (x, weights, weights, weights, weights, *[g[None] for g in gains], cosine, sine, segs[:, None], segs.reshape(-1, 1, LEN))


def attention(inputs):
    x, weights = inputs[:2]
    count = x.shape[0]
    in_specs, saved, token = attention_specs(weights)[:3]
    wide = HEADS * HD
    shapes = [(wide, F32), (HD, F32), (wide, BF16), (HD, BF16), (HD, BF16), (wide, BF16), (D, F32), (D, F32)]
    return pl.pallas_call(
        attention_kernel,
        grid=(count // LEN, HEADS),
        in_specs=in_specs,
        out_specs=[*saved, token],
        out_shape=[jax.ShapeDtypeStruct((count, width), kind) for width, kind in shapes],
        scratch_shapes=[pltpu.VMEM((LEN, D), BF16)],
        compiler_params=pltpu.CompilerParams(vmem_limit_bytes=60 << 20),
        cost_estimate=pl.CostEstimate(flops=count * (4 * D * 1280 + 4096 * 576), bytes_accessed=count * 16384, transcendentals=count * 2304),
    )(*inputs)


def attention_back(inputs, saved, d_middle):
    x, weights = inputs[:2]
    count = x.shape[0]
    rows, cols, depth, _ = weights.shape
    in_specs, saved_specs, token, heads, share, fixed = attention_specs(weights)
    wide_grad = jax.ShapeDtypeStruct((rows, cols, depth, HEADS // cols * HD), BF16)
    narrow_grad = jax.ShapeDtypeStruct((rows, cols, depth, HD // cols), BF16)
    gains = [D, D, HD, HD]
    return pl.pallas_call(
        attention_back_kernel,
        grid=(count // LEN, HEADS),
        in_specs=[*in_specs, *saved_specs, token],
        out_specs=[heads(0), share(0), share(0), heads(0), token, *[fixed(g) for g in gains]],
        out_shape=[
            wide_grad, narrow_grad, narrow_grad, wide_grad,
            jax.ShapeDtypeStruct((count, D), BF16),
            *[jax.ShapeDtypeStruct((1, g), F32) for g in gains],
        ],
        scratch_shapes=[
            pltpu.VMEM((LEN, D), BF16),
            pltpu.VMEM((LEN, D), BF16),
            pltpu.VMEM((LEN, HD), F32),
            pltpu.VMEM((LEN, HD), F32),
            pltpu.VMEM((LEN, HD), F32),
            pltpu.VMEM((LEN, D), F32),
            pltpu.VMEM((LEN, HD), BF16),
        ],
        compiler_params=pltpu.CompilerParams(vmem_limit_bytes=60 << 20),
        cost_estimate=pl.CostEstimate(flops=count * (8 * D * 1280 + 10240 * 576), bytes_accessed=count * 20000, transcendentals=count * 2304),
    )(*inputs, *saved, d_middle)


CHUNK = 512


def ffn_kernel(
    middle_ref, e0_ref, wg_ref, wu_ref, wd_ref, g_pre, g_ffn,
    out_ref, d_middle_ref, gg_ffn_ref, gg_pre_ref, gw_gate, gw_up, gw_down,
    a2_s, gate_s, up_s, hidden_s, yf_s, dyf_s,
):
    second, chunk = pl.program_id(0) == 1, pl.program_id(1)
    last = chunk == pl.num_programs(1) - 1

    @pl.when(jnp.logical_not(second) & (chunk == 0))
    def _():
        middle = middle_ref[...]
        a2_s[...] = (middle * inverse_rms(middle) * g_pre[...]).astype(BF16)
        yf_s[...] = jnp.zeros_like(yf_s)

    @pl.when(jnp.logical_not(second))
    def _():
        a2 = a2_s[...]
        gate = dot(a2, joined(wg_ref))
        up = dot(a2, joined(wu_ref))
        gate_s[chunk] = gate
        up_s[chunk] = up
        hidden = (jax.nn.gelu(gate, approximate=True) * up).astype(BF16)
        hidden_s[chunk] = hidden
        yf_s[...] += dot_cols(hidden, joined(wd_ref))

    @pl.when(jnp.logical_not(second) & last)
    def _():
        y_f, e0 = yf_s[...], e0_ref[...].astype(F32)
        inv = inverse_rms(y_f)
        out_ref[...] = (middle_ref[...] + y_f * inv * g_ffn[...]).astype(BF16)
        dyf_s[...] = norm_back(y_f, inv, g_ffn[...], e0).astype(BF16)
        gg_ffn_ref[...] = gain_back(y_f, inv, e0)[None]
        yf_s[...] = jnp.zeros_like(yf_s)

    @pl.when(second)
    def _():
        d_yf, a2 = dyf_s[...], a2_s[...]
        gate, up = gate_s[chunk], up_s[chunk]
        d_hidden = dot(d_yf, joined(wd_ref))
        square = gate * gate
        inner = GELU_C * gate * (1.0 + 0.044715 * square)
        tanh = jnp.tanh(inner)
        half = 0.5 * (1.0 + tanh)
        slope = half + 0.5 * gate * (1.0 - tanh * tanh) * (GELU_C * (1.0 + 0.134145 * square))
        d_gate = (d_hidden * up * slope).astype(BF16)
        d_up = (d_hidden * (gate * half)).astype(BF16)
        gw_gate[...] = dot_rows(a2, d_gate).astype(BF16).reshape(gw_gate.shape)
        gw_up[...] = dot_rows(a2, d_up).astype(BF16).reshape(gw_up.shape)
        gw_down[...] = dot_rows(d_yf, hidden_s[chunk]).astype(BF16).reshape(gw_down.shape)
        yf_s[...] += dot_cols(d_gate, joined(wg_ref)) + dot_cols(d_up, joined(wu_ref))

    @pl.when(second & last)
    def _():
        middle, d_a2 = middle_ref[...], yf_s[...]
        inv = inverse_rms(middle)
        d_middle_ref[...] = e0_ref[...].astype(F32) + norm_back(middle, inv, g_pre[...], d_a2)
        gg_pre_ref[...] = gain_back(middle, inv, d_a2)[None]


GELU_C = math.sqrt(2.0 / math.pi)


def ffn(middle, e0, weights, g_pre, g_ffn):
    count = middle.shape[0]
    rows, cols, depth = weights.shape[:3]
    width = weights.shape[3] // 3
    per = width // CHUNK
    chunks = cols * per
    once = pl.Buffered(1)

    def weight(which):
        return pl.BlockSpec((rows, 1, depth, CHUNK), lambda p, t: (0, t // per, 0, which * per + t % per))

    def whole(shape):
        return pl.BlockSpec(shape, lambda p, t: (0, 0), pipeline_mode=once)

    grad = pl.BlockSpec((rows, 1, depth, CHUNK), lambda p, t: (0, (p * t) // per, 0, (p * t) % per))
    grad_shape = jax.ShapeDtypeStruct((rows, cols, depth, width), BF16)
    return pl.pallas_call(
        ffn_kernel,
        grid=(2, chunks),
        in_specs=[whole((count, D)), whole((count, D)), weight(0), weight(1), weight(2), whole((1, D)), whole((1, D))],
        out_specs=[whole((count, D)), whole((count, D)), whole((1, D)), whole((1, D)), grad, grad, grad],
        out_shape=[
            jax.ShapeDtypeStruct((count, D), BF16),
            jax.ShapeDtypeStruct((count, D), F32),
            jax.ShapeDtypeStruct((1, D), F32),
            jax.ShapeDtypeStruct((1, D), F32),
            grad_shape, grad_shape, grad_shape,
        ],
        scratch_shapes=[
            pltpu.VMEM((count, D), BF16),
            pltpu.VMEM((chunks, count, CHUNK), F32),
            pltpu.VMEM((chunks, count, CHUNK), F32),
            pltpu.VMEM((chunks, count, CHUNK), BF16),
            pltpu.VMEM((count, D), F32),
            pltpu.VMEM((count, D), BF16),
        ],
        compiler_params=pltpu.CompilerParams(vmem_limit_bytes=60 << 20),
        cost_estimate=pl.CostEstimate(flops=18 * count * D * FF, bytes_accessed=36 * D * FF, transcendentals=2 * count * FF),
    )(middle, e0, weights, weights, weights, g_pre[None], g_ffn[None])


def local(
    tokens,
    w_query,
    w_key,
    w_value,
    w_out,
    w_gate,
    w_up,
    w_down,
    gain_input,
    gain_post_attn,
    gain_pre_ffn,
    gain_post_ffn,
    gain_query,
    gain_key,
    segment_ids,
    positions,
    cotangent,
):
    rows, cols = lax.axis_size("row"), lax.axis_size("col")
    place = lax.axis_index("row") * cols + lax.axis_index("col")
    count = tokens.shape[0] // (rows * cols)
    assert count == LEN
    width = gain_input.shape[0]
    wide, narrow, ff_width = w_query.shape[1], w_key.shape[1], w_gate.shape[1]

    gains = lax.all_gather(
        jnp.stack([gain_input, gain_post_attn, gain_pre_ffn, gain_post_ffn]), GROUP, axis=1, tiled=True
    )
    attn_w = gather_blocks(jnp.concatenate([w_query, w_key, w_value, w_out.T], axis=1))
    x = to_tokens(tokens)
    ffn_w = gather_blocks(jnp.concatenate([w_gate, w_up, w_down.T], axis=1))
    e0 = to_tokens(cotangent)
    segs = lax.dynamic_slice_in_dim(segment_ids, place * count, count)
    cosine, sine = rotary_tables(lax.dynamic_slice_in_dim(positions, place * count, count))

    inputs = attention_inputs(
        x, attn_w, (gains[0], gains[1], gain_query, gain_key), cosine, sine, segs
    )
    *saved, middle = attention(inputs)
    result, d_middle, gg_ffn, gg_pre, gw_gate, gw_up, gw_down = ffn(
        middle, e0, ffn_w, gains[2], gains[3]
    )
    ffn_own = scatter_blocks(jnp.concatenate([gw_gate, gw_up, gw_down], axis=3))
    output = to_features(result)
    gw_q, gw_k, gw_v, gw_o, grad_x, gg_in, gg_attn, gg_query, gg_key = attention_back(
        inputs, saved, d_middle
    )
    gw_attn, ffn_own = lax.optimization_barrier(
        (jnp.concatenate([gw_q, gw_k, gw_v, gw_o], axis=3), ffn_own)
    )
    attn_own = scatter_blocks(gw_attn)
    ffn_grads = lax.psum(ffn_own, "dp")
    ffn_grads, attn_own = lax.optimization_barrier((ffn_grads, attn_own))
    ffn_grads = ffn_grads.astype(F32)
    attn_grads = lax.psum(attn_own, "dp").astype(F32)
    grad_tokens = to_features(grad_x)

    sums = lax.psum(
        jnp.concatenate([gg_in, gg_attn, gg_pre, gg_ffn, gg_query, gg_key], axis=1)[0],
        ("dp", "row", "col"),
    )
    own = lax.dynamic_slice_in_dim(sums[: 4 * D].reshape(4, D), place * width, width, 1)
    return (
        output,
        grad_tokens,
        attn_grads[:, :wide],
        attn_grads[:, wide : wide + narrow],
        attn_grads[:, wide + narrow : wide + 2 * narrow],
        attn_grads[:, wide + 2 * narrow :].T,
        ffn_grads[:, :ff_width],
        ffn_grads[:, ff_width : 2 * ff_width],
        ffn_grads[:, 2 * ff_width :].T,
        own[0],
        own[1],
        own[2],
        own[3],
        sums[4 * D : 4 * D + HD],
        sums[4 * D + HD :],
    )


def solution(mesh):
    tokens, block, turned, gain = P("dp", GROUP), P("row", "col"), P("col", "row"), P(GROUP)
    in_specs = (
        tokens, block, block, block, turned, block, block, turned,
        gain, gain, gain, gain, P(), P(), P("dp"), P("dp"), tokens,
    )
    out_specs = (
        tokens, tokens, block, block, block, turned, block, block, turned,
        gain, gain, gain, gain, P(), P(),
    )
    return jax.shard_map(local, mesh=mesh, in_specs=in_specs, out_specs=out_specs, check_vma=False)
```

time: 2070 us -> 465 us (0.22)
  waiting for transfers between devices: 1460 us -> 239 us
  blocking collectives: 248 us -> 56.2 us
  matrix products: 189 us -> 0 us
  other arithmetic: 120 us -> 19.2 us
  Pallas kernels: 0 us -> 97.7 us
    reduce_scatter x9 -> x2, waiting for transfers between devices: 740 us -> 75.6 us  [scatter_blocks(): return lax.psum_scatter(blocks, GROUP, scatter_dimension=0)]
    all_gather x11 -> x2, waiting for transfers between devices: 456 us -> 13.5 us  [gather_blocks(): return lax.all_gather(block, GROUP).reshape(rows, cols, *block.shape)]
    psum x11 -> x1, blocking collectives: 248 us -> 39.8 us  [local(): lax.psum(jnp.concatenate([gg_in, gg_attn, gg_pre, gg_ffn, gg_query, gg_ke...]
    dot_general x49 -> x0, matrix products: 189 us -> none  [the longest x7 46.4 us: contract_cols(): lax.dot_general(left, right, (((1,), (1,)), ((), ())), preferred_element_...]
    psum x3 -> x2, waiting for transfers between devices: 262 us -> 106 us  [the longest x1 74.1 us: local(): ffn_grads = lax.psum(ffn_own, 'dp')]
    pallas_call x0 -> x3, Pallas kernels: none -> 97.7 us  [the longest x1 42.7 us: ffn(): pl.pallas_call(ffn_kernel, grid=(2, chunks), in_specs=[whole((count, D)),...]
    convert_element_type x16 -> x3, other arithmetic: 56.5 us -> 2.48 us  [the longest x1 1.33 us: local(): attn_grads = lax.psum(attn_own, 'dp').astype(F32)]
    all_to_all x0 -> x4, waiting for transfers between devices: none -> 43.5 us  [the longest x2 27.8 us: to_tokens(): return lax.all_to_all(block, GROUP, split_axis=0, concat_axis=1, tiled=True)]
  transfers between devices with their start and end apart: 23 -> 10, of which waited for: 20 -> 7; matrix products, arithmetic and copies ran while one was open for 5% -> 6% of each run, Pallas kernels for 0% -> 12%
where the time goes in v1:
time: 465 us; the launch traced here: 464 us
  waiting for transfers between devices  239 us (51%)
  Pallas kernels  97.7 us (21%)
  blocking collectives  56.2 us (12%)
  local copies, waits for them, and re-layouts  21.5 us (5%)
  other arithmetic  19.2 us (4%)
  starting transfers between devices  15.9 us (3%)
  between operations  14.4 us (3%)
    reduce_scatter x2, waiting for transfers between devices, scatter_blocks(): return lax.psum_scatter(blocks, GROUP, scatter_dimension=0)  75.6 us
    psum x1, waiting for transfers between devices, local(): ffn_grads = lax.psum(ffn_own, 'dp')  74.1 us
    pallas_call x1, Pallas kernels, ffn(): pl.pallas_call(ffn_kernel, grid=(2, chunks), in_specs=[whole((count, D)),...  42.7 us
    psum x1, blocking collectives, local(): lax.psum(jnp.concatenate([gg_in, gg_attn, gg_pre, gg_ffn, gg_query, gg_ke...  39.8 us
    pallas_call x1, Pallas kernels, attention_back(): pl.pallas_call(attention_back_kernel, grid=(count // LEN, HEADS), in_spec...  32.3 us
    psum x1, waiting for transfers between devices, local(): attn_grads = lax.psum(attn_own, 'dp').astype(F32)  31.9 us
    all_to_all x2, waiting for transfers between devices, to_tokens(): return lax.all_to_all(block, GROUP, split_axis=0, concat_axis=1, tiled=True)  27.8 us
    pallas_call x1, Pallas kernels, attention(): pl.pallas_call(attention_kernel, grid=(count // LEN, HEADS), in_specs=in_...  22.7 us
  transfers between devices with their start and end apart: 10, of which 7 were waited for; matrix products, arithmetic and copies ran while one was open for 6% of the time, Pallas kernels for 12%

profile of v1, /device:TPU:0, one launch (start us, length us, event | category | flops | bytes accessed | tf_op | source)
XLA Modules:
  0.0 464.2 jit_solution(6182882112775958374)
XLA Ops:
  7.3 2.2 pad_maximum_fusion.3
  12.7 4.2 all-to-all-start
  18.1 27.8 %all-to-all-done = bf16[4,1024,160]{1,2,0:T(8,128)(2,1)S(1)} async-done(((bf16[4,1024,160]{1,2,0:T(8,128)(2,1)}), bf16[4,1024,160]{1,2,0:T(8,128)(2,1)S(1)}, u32[]{:S(2)}, u32[]{:S(2)}) %all-to-all-start) | async-done | bytes 1310752 | tf_op jit(solution)/shard_map/all_to_all | solution.py:69
  45.9 3.6 all-to-all-start.1
  51.3 16.4 %all-gather.2 = f32[4,160,4]{1,2,0:T(4,128)S(1)} all-gather(f32[1,160,4]{1,2,0:T(4,128)S(1)} %maximum_bitcast_fusion), channel_id=1, replica_groups=mesh['dp'=8,'row'=2,'col'=2] {'row','col'}, dimensions={0}, use_global_device_ids=true | all-gather | bytes 12800 | tf_op jit(solution)/shard_map/all_gather | solution.py:429
  69.1 3.0 multiply_sine_fusion
  75.0 22.7 %shard_map.280 = (f32[1024,1024]{1,0:T(8,128)}, f32[1024,256]{1,0:T(8,128)}, bf16[1024,1024]{1,0:T(8,128)(2,1)}, bf16[1024,256]{1,0:T(8,128)(2,1)}, bf16[1024,25...) custom-call(bf16[1024,640]{1,0:T(8,128)(2,1)} %copy.56.x_ref, ...), custom_call_target="tpu_custom_call" | custom-call | flops 5771362304 | bytes 16777216 | tf_op jit(solution)/shard_map/pallas_call | solution.py:253
  97.7 13.5 %all-gather.8.cloned.1.call-done = bf16[1280,3072]{1,0:T(8,128)(2,1)} async-done(((bf16[320,3072]{1,0:T(8,128)(2,1)}), bf16[1280,3072]{1,0:T(8,128)(2,1)}) %all-gather.8.cloned.1.call-update) | async-done | bytes 7864336 | tf_op jit(solution)/shard_map/all_gather | solution.py:60
  111.3 42.7 %shard_map.281 = (bf16[1024,640]{1,0:T(8,128)(2,1)}, f32[1024,640]{1,0:T(8,128)}, f32[1,640]{1,0:T(1,128)}, f32[1,640]{1,0:T(1,128)}, bf16[2,2,320,1024]{3,2,1,0...) custom-call(f32[1024,640]{1,0:T(8,128)} %get-tuple-element.43.middle_ref, ...), custom_call_target="tpu_custom_call" | custom-call | flops 24159191040 | bytes 47185920 | tf_op jit(solution)/shard_map/pallas_call | solution.py:378
  154.0 6.7 %pad_maximum_fusion = bf16[2,2,320,3072]{3,2,1,0:T(8,128)(2,1)} fusion(bf16[2,2,320,1024]{3,2,1,0:T(8,128)(2,1)} %get-tuple-element.60, bf16[2,2,320,1024]{3,2,1,0:T(8,128)(2,1)} %get-tuple-element.59, bf16[2,2,320,1024]{3,2,1,0:T(8,128)(2,1)} %get-tuple-element.58), kind=kLoop, calls=%fused_computation | loop fusion | flops 23592960 | bytes 15728640 | tf_op jit(solution)/shard_map/concatenate | solution.py:446
  160.7 32.3 %shard_map.282 = (bf16[2,2,320,512]{3,2,1,0:T(8,128)(2,1)}, bf16[2,2,320,128]{3,2,1,0:T(8,128)(2,1)}, bf16[2,2,320,128]{3,2,1,0:T(8,128)(2,1)}, bf16[2,2,320,512...) custom-call(bf16[1024,640]{1,0:T(8,128)(2,1)} %copy.56.x_ref, ...), custom_call_target="tpu_custom_call" | custom-call | flops 12750684160 | bytes 20480000 | tf_op jit(solution)/shard_map/pallas_call | solution.py:273
  193.0 3.3 pad_maximum_fusion.1
  196.4 34.7 %reduce-scatter.3.cloned.1.call-done = bf16[1,320,3072]{2,1,0:T(8,128)(2,1)} async-done(((bf16[4,320,3072]{2,1,0:T(8,128)(2,1)}), bf16[1,320,3072]{2,1,0:T(8,128)(2,1)}) %reduce-scatter.3.cloned.1.call-update) | async-done | bytes 1966096 | tf_op jit(solution)/shard_map/reduce_scatter | solution.py:65
  232.4 1.5 copy.64
  233.9 3.5 all-to-all-start.3
  237.5 1.5 copy.60
  239.0 15.7 %all-to-all-done.3 = bf16[1024,4,160]{0,2,1:T(8,128)(2,1)S(1)} async-done(((bf16[1024,4,160]{0,2,1:T(8,128)(2,1)}), bf16[1024,4,160]{0,2,1:T(8,128)(2,1)S(1)}, u32[]{:S(2)}, u32[]{:S(2)}) %all-to-all-start.3) | async-done | bytes 1310752 | tf_op jit(solution)/shard_map/all_to_all | solution.py:73
  254.7 4.3 all-to-all-start.2
  259.1 74.1 %all-reduce.3.cloned.1.call-done = bf16[320,3072]{1,0:T(8,128)(2,1)} async-done(((bf16[320,3072]{1,0:T(8,128)(2,1)}), bf16[320,3072]{1,0:T(8,128)(2,1)}) %all-reduce.3.cloned.1.call-update) | async-done | bytes 1966096 | tf_op jit(solution)/shard_map/psum | solution.py:455
  333.2 40.9 %reduce-scatter.5.cloned.1.call-done = bf16[1,320,1280]{2,1,0:T(8,128)(2,1)} async-done(((bf16[4,320,1280]{2,1,0:T(8,128)(2,1)}), bf16[1,320,1280]{2,1,0:T(8,128)(2,1)}) %reduce-scatter.5.cloned.1.call-update) | async-done | bytes 819216 | tf_op jit(solution)/shard_map/reduce_scatter | solution.py:65
  374.2 39.8 %psum.23 = f32[3072]{0:T(1024)S(1)} all-reduce(f32[3072]{0:T(1024)S(1)} %bitcast.70), channel_id=1, replica_groups=mesh['dp'=8,'row'=2,'col'=2] {'dp','row','col'}, use_global_device_ids=true, to_apply=%region_4.0 | all-reduce | flops 3072 | bytes 24576 | tf_op jit(solution)/shard_map/psum | solution.py:461
  416.4 2.5 copy.68
  419.4 2.1 fusion
  421.5 31.9 %all-reduce.5.cloned.1.call-done = bf16[320,1280]{1,0:T(8,128)(2,1)} async-done(((bf16[320,1280]{1,0:T(8,128)(2,1)}), bf16[320,1280]{1,0:T(8,128)(2,1)}) %all-reduce.5.cloned.1.call-update) | async-done | bytes 819216 | tf_op jit(solution)/shard_map/psum | solution.py:458
  (83 shorter events, 18.8 us)
Async XLA Ops:
  7.2 67.8 %all-gather.6.cloned.1.call-start = ((), (), s32[]{:S(2)}) async-start(), calls=%async_computation.10 | async-start | bytes 4096000 | tf_op jit(solution)/shard_map/all_gather | solution.py:60
  9.5 101.7 %all-gather.8.cloned.1.call-start = ((), (), s32[]{:S(2)}) async-start(), calls=%async_computation.11 | async-start | bytes 9830400 | tf_op jit(solution)/shard_map/all_gather | solution.py:60
  11.5 5.4 %copy-start.3 = (bf16[4096,160]{0,1:T(8,128)(2,1)S(1)}, bf16[4096,160]{0,1:T(8,128)(2,1)}, u32[]{:S(2)}) copy-start(bf16[4096,160]{0,1:T(8,128)(2,1)} %param.33) | copy-start | bytes 3932164
  12.7 33.2 %all-to-all-start = ((bf16[4,1024,160]{1,2,0:T(8,128)(2,1)}), bf16[4,1024,160]{1,2,0:T(8,128)(2,1)S(1)}, u32[]{:S(2)}, u32[]{:S(2)}) async-start(bf16[4,1024,160]{1,2,0:T(8,128)(2,1)} %bitcast.53), calls=%async_computation | async-start | bytes 2621440 | tf_op jit(solution)/shard_map/all_to_all | solution.py:69
  18.1 33.2 %copy-start.16 = (f32[160]{0:T(256)S(1)}, f32[160]{0:T(256)}, u32[]{:S(2)}) copy-start(f32[160]{0:T(256)} %param.28) | copy-start | bytes 1924
  18.1 33.2 %copy-start.17 = (f32[160]{0:T(256)S(1)}, f32[160]{0:T(256)}, u32[]{:S(2)}) copy-start(f32[160]{0:T(256)} %param.27) | copy-start | bytes 1924
  18.1 33.2 %copy-start.18 = (f32[160]{0:T(256)S(1)}, f32[160]{0:T(256)}, u32[]{:S(2)}) copy-start(f32[160]{0:T(256)} %param.26) | copy-start | bytes 1924
  18.1 33.2 %copy-start.19 = (f32[160]{0:T(256)S(1)}, f32[160]{0:T(256)}, u32[]{:S(2)}) copy-start(f32[160]{0:T(256)} %param.25) | copy-start | bytes 1924
  45.9 27.7 %all-to-all-start.1 = ((bf16[4,1024,160]{1,2,0:T(8,128)(2,1)}), bf16[4,1024,160]{1,2,0:T(8,128)(2,1)S(1)}, u32[]{:S(2)}, u32[]{:S(2)}) async-start(bf16[4,1024,160]{1,2,0:T(8,128)(2,1)} %bitcast.52), calls=%async_computation.1 | async-start | bytes 2621440 | tf_op jit(solution)/shard_map/all_to_all | solution.py:69
  49.5 181.6 %reduce-scatter.3.cloned.1.call-start = ((), (), s32[]{:S(2)}) async-start(), calls=%async_computation.6 | async-start | bytes 9830400 | tf_op jit(solution)/shard_map/reduce_scatter | solution.py:65
  50.2 23.4 %copy-start.9 = (s32[1024]{0:T(1024)}, s32[1024]{0:T(1024)S(1)}, u32[]{:S(2)}) copy-start(s32[1024]{0:T(1024)S(1)} %dynamic_slice.10) | copy-start | bytes 12292
  160.7 172.6 %all-reduce.3.cloned.1.call-start = ((), (), s32[]{:S(2)}) async-start(), calls=%async_computation.7 | async-start | bytes 3932160 | tf_op jit(solution)/shard_map/psum | solution.py:455
  231.1 143.0 %reduce-scatter.5.cloned.1.call-start = ((), (), s32[]{:S(2)}) async-start(), calls=%async_computation.8 | async-start | bytes 4096000 | tf_op jit(solution)/shard_map/reduce_scatter | solution.py:65
  232.4 5.0 %copy-start.4 = (bf16[1024,640]{1,0:T(8,128)(2,1)S(1)}, bf16[1024,640]{1,0:T(8,128)(2,1)}, u32[]{:S(2)}) copy-start(bf16[1024,640]{1,0:T(8,128)(2,1)} %get-tuple-element.44) | copy-start | bytes 3932164
  233.9 20.8 %all-to-all-start.3 = ((bf16[1024,4,160]{0,2,1:T(8,128)(2,1)}), bf16[1024,4,160]{0,2,1:T(8,128)(2,1)S(1)}, u32[]{:S(2)}, u32[]{:S(2)}) async-start(bf16[1024,4,160]{0,2,1:T(8,128)(2,1)} %bitcast.21), calls=%async_computation.3 | async-start | bytes 2621440 | tf_op jit(solution)/shard_map/all_to_all | solution.py:73
  237.4 21.6 %copy-start.13 = (f32[1,640]{1,0:T(1,128)S(1)}, f32[1,640]{1,0:T(1,128)}, u32[]{:S(2)}) copy-start(f32[1,640]{1,0:T(1,128)} %get-tuple-element.65) | copy-start | bytes 7684
  237.5 21.6 %copy-start.12 = (f32[1,640]{1,0:T(1,128)S(1)}, f32[1,640]{1,0:T(1,128)}, u32[]{:S(2)}) copy-start(f32[1,640]{1,0:T(1,128)} %get-tuple-element.66) | copy-start | bytes 7684
  237.5 21.6 %copy-start.11 = (f32[1,640]{1,0:T(1,128)S(1)}, f32[1,640]{1,0:T(1,128)}, u32[]{:S(2)}) copy-start(f32[1,640]{1,0:T(1,128)} %get-tuple-element.67) | copy-start | bytes 7684
  237.5 21.6 %copy-start.10 = (f32[1,640]{1,0:T(1,128)S(1)}, f32[1,640]{1,0:T(1,128)}, u32[]{:S(2)}) copy-start(f32[1,640]{1,0:T(1,128)} %get-tuple-element.68) | copy-start | bytes 7684
  237.5 21.6 %copy-start.15 = (f32[1,256]{1,0:T(1,128)S(1)}, f32[1,256]{1,0:T(1,128)}, u32[]{:S(2)}) copy-start(f32[1,256]{1,0:T(1,128)} %get-tuple-element.69) | copy-start | bytes 3076
  239.0 135.2 %copy-start.14 = (f32[1,256]{1,0:T(1,128)S(1)}, f32[1,256]{1,0:T(1,128)}, u32[]{:S(2)}) copy-start(f32[1,256]{1,0:T(1,128)} %get-tuple-element.70) | copy-start | bytes 3076
  254.7 161.8 %all-to-all-start.2 = ((bf16[1024,4,160]{0,2,1:T(8,128)(2,1)}), bf16[1024,4,160]{0,2,1:T(8,128)(2,1)}, u32[]{:S(2)}, u32[]{:S(2)}) async-start(bf16[1024,4,160]{0,2,1:T(8,128)(2,1)} %bitcast.19), calls=%async_computation.2 | async-start | bytes 2621440 | tf_op jit(solution)/shard_map/all_to_all | solution.py:73
  259.0 194.4 %all-reduce.5.cloned.1.call-start = ((), (), s32[]{:S(2)}) async-start(), calls=%async_computation.9 | async-start | bytes 1638400 | tf_op jit(solution)/shard_map/psum | solution.py:458
  415.3 3.7 copy-start
  (6 other events, 12.6 us)
Sparse Core Ops, SparseCore 0:
  10.2 43.0 all-gather.5
  54.9 56.3 all-gather.7
  160.8 70.2 reduce-scatter.2
  234.9 98.2 all-reduce.2
  335.7 38.4 reduce-scatter.4
  377.9 75.5 all-reduce.4

commit v2 on v1

--- a/solution.py
+++ b/solution.py
@@ -60,17 +60,84 @@
     return lax.all_gather(block, GROUP).reshape(rows, cols, *block.shape)
 
 
+def col_first(grads):
+    return jnp.concatenate([g.transpose(1, 0, 2, 3) for g in grads], axis=3)
+
+
+def neighbours(axis, mask):
+    return [(i, i ^ mask) for i in range(lax.axis_size(axis))]
+
+
+def halve(value, axis, mask):
+    size = value.shape[0] // 2
+    bit = (lax.axis_index(axis) // mask) % 2
+    sent = lax.dynamic_slice_in_dim(value, (1 - bit) * size, size, 0)
+    kept = lax.dynamic_slice_in_dim(value, bit * size, size, 0)
+    got = lax.ppermute(sent, axis, neighbours(axis, mask))
+    return (kept.astype(F32) + got.astype(F32)).astype(BF16)
+
+
+def double(value, axis, mask):
+    bit = (lax.axis_index(axis) // mask) % 2
+    got = lax.ppermute(value, axis, neighbours(axis, mask))
+    return jnp.concatenate([jnp.where(bit == 0, value, got), jnp.where(bit == 0, got, value)], axis=0)
+
+
 def scatter_blocks(blocks):
-    blocks = blocks.reshape(-1, *blocks.shape[2:])
-    return lax.psum_scatter(blocks, GROUP, scatter_dimension=0)
+    return halve(halve(blocks, "col", 1)[0], "row", 1)[0]
+
+
+def masks(axis):
+    size = lax.axis_size(axis)
+    return [1 << bit for bit in range(size.bit_length() - 1)]
+
+
+def total_halving(value):
+    for mask in masks("dp"):
+        value = halve(value, "dp", mask)
+    for mask in reversed(masks("dp")):
+        value = double(value, "dp", mask)
+    return value
+
+
+def total_small(value):
+    for axis in ("col", "row", "dp"):
+        for mask in masks(axis):
+            value = value + lax.ppermute(value, axis, neighbours(axis, mask))
+    return value
+
+
+def partners():
+    rows, cols = lax.axis_size("row"), lax.axis_size("col")
+    place = lax.axis_index("row") * cols + lax.axis_index("col")
+    count = rows * cols
+    swaps = [[(i, i ^ mask) for i in range(count)] for mask in range(count)]
+    return place, count, swaps
+
+
+def by_place(parts, place):
+    stacked = jnp.stack(parts)
+    return [lax.dynamic_index_in_dim(stacked, place ^ j, 0, keepdims=False) for j in range(len(parts))]
+
+
+def swap(part, perm):
+    return lax.ppermute(part, GROUP, perm)
 
 
 def to_tokens(block):
-    return lax.all_to_all(block, GROUP, split_axis=0, concat_axis=1, tiled=True)
+    place, count, swaps = partners()
+    size = block.shape[0] // count
+    parts = [lax.dynamic_slice_in_dim(block, (place ^ m) * size, size, 0) for m in range(count)]
+    parts = parts[:1] + [swap(parts[m], swaps[m]) for m in range(1, count)]
+    return jnp.concatenate(by_place(parts, place), axis=1)
 
 
 def to_features(block):
-    return lax.all_to_all(block, GROUP, split_axis=1, concat_axis=0, tiled=True)
+    place, count, swaps = partners()
+    size = block.shape[1] // count
+    parts = [lax.dynamic_slice_in_dim(block, (place ^ m) * size, size, 1) for m in range(count)]
+    parts = parts[:1] + [swap(parts[m], swaps[m]) for m in range(1, count)]
+    return jnp.concatenate(by_place(parts, place), axis=0)
 
 
 BLOCK = 256
@@ -443,24 +510,19 @@
     result, d_middle, gg_ffn, gg_pre, gw_gate, gw_up, gw_down = ffn(
         middle, e0, ffn_w, gains[2], gains[3]
     )
-    ffn_own = scatter_blocks(jnp.concatenate([gw_gate, gw_up, gw_down], axis=3))
+    ffn_own = scatter_blocks(col_first([gw_gate, gw_up, gw_down]))
     output = to_features(result)
     gw_q, gw_k, gw_v, gw_o, grad_x, gg_in, gg_attn, gg_query, gg_key = attention_back(
         inputs, saved, d_middle
     )
-    gw_attn, ffn_own = lax.optimization_barrier(
-        (jnp.concatenate([gw_q, gw_k, gw_v, gw_o], axis=3), ffn_own)
-    )
-    attn_own = scatter_blocks(gw_attn)
-    ffn_grads = lax.psum(ffn_own, "dp")
-    ffn_grads, attn_own = lax.optimization_barrier((ffn_grads, attn_own))
-    ffn_grads = ffn_grads.astype(F32)
-    attn_grads = lax.psum(attn_own, "dp").astype(F32)
+    attn_grads = total_halving(
+        scatter_blocks(col_first([gw_q, gw_k, gw_v, gw_o]))
+    ).astype(F32)
+    ffn_grads = lax.psum(ffn_own, "dp").astype(F32)
     grad_tokens = to_features(grad_x)
 
-    sums = lax.psum(
-        jnp.concatenate([gg_in, gg_attn, gg_pre, gg_ffn, gg_query, gg_key], axis=1)[0],
-        ("dp", "row", "col"),
+    sums = total_small(
+        jnp.concatenate([gg_in, gg_attn, gg_pre, gg_ffn, gg_query, gg_key], axis=1)[0]
     )
     own = lax.dynamic_slice_in_dim(sums[: 4 * D].reshape(4, D), place * width, width, 1)
     return (

time: 465 us -> 458 us (0.985); the launches traced: 464 us -> 449 us
  waiting for transfers between devices: 239 us -> 190 us
  other arithmetic: 19.2 us -> 43.6 us
  blocking collectives: 56.2 us -> 39.4 us
  local copies, waits for them, and re-layouts: 21.5 us -> 37.3 us
  starting transfers between devices: 15.9 us -> 26.4 us
    ppermute x0 -> x27, waiting for transfers between devices: none -> 94.5 us  [the longest x7 33.5 us: halve(): got = lax.ppermute(sent, axis, neighbours(axis, mask))]
    reduce_scatter x2 -> x0, waiting for transfers between devices: 75.6 us -> none  [scatter_blocks(): return lax.psum_scatter(blocks, GROUP, scatter_dimension=0)]
    all_to_all x4 -> x0, waiting for transfers between devices: 43.5 us -> none  [the longest x2 27.8 us: to_tokens(): return lax.all_to_all(block, GROUP, split_axis=0, concat_axis=1, tiled=True)]
    psum x1 -> x0, blocking collectives: 39.8 us -> none  [local(): lax.psum(jnp.concatenate([gg_in, gg_attn, gg_pre, gg_ffn, gg_query, gg_ke...]
    ppermute x0 -> x27, starting transfers between devices: none -> 26.3 us  [the longest x12 10.5 us: swap(): return lax.ppermute(part, GROUP, perm)]
    psum x2 -> x1, waiting for transfers between devices: 106 us -> 79.9 us  [local(): ffn_grads = lax.psum(ffn_own, 'dp').astype(F32)]
    all_gather x1, blocking collectives: 16.4 us -> 39.4 us  [local(): lax.all_gather(jnp.stack([gain_input, gain_post_attn, gain_pre_ffn, gain_...]
    dynamic_slice x0 -> x26, local copies, waits for them, and re-layouts: none -> 19.4 us  [the longest x19 12.6 us: by_place(): lax.dynamic_index_in_dim(stacked, place ^ j, 0, keepdims=False)]
  transfers between devices with their start and end apart: 10 -> 30, of which waited for: 7 -> 12; matrix products, arithmetic and copies ran while one was open for 6% -> 13% of each run, Pallas kernels for 12% -> 5%
where the time goes in v2:
time: 458 us; the launch traced here: 449 us
  waiting for transfers between devices  190 us (41%)
  Pallas kernels  97.9 us (21%)
  other arithmetic  43.6 us (10%)
  blocking collectives  39.4 us (9%)
  local copies, waits for them, and re-layouts  37.3 us (8%)
  starting transfers between devices  26.4 us (6%)
  between operations  14.7 us (3%)
    psum x1, waiting for transfers between devices, local(): ffn_grads = lax.psum(ffn_own, 'dp').astype(F32)  79.9 us
    pallas_call x1, Pallas kernels, ffn(): pl.pallas_call(ffn_kernel, grid=(2, chunks), in_specs=[whole((count, D)),...  42.9 us
    all_gather x1, blocking collectives, local(): lax.all_gather(jnp.stack([gain_input, gain_post_attn, gain_pre_ffn, gain_...  39.4 us
    ppermute x7, waiting for transfers between devices, halve(): got = lax.ppermute(sent, axis, neighbours(axis, mask))  33.5 us
    pallas_call x1, Pallas kernels, attention_back(): pl.pallas_call(attention_back_kernel, grid=(count // LEN, HEADS), in_spec...  32.2 us
    pallas_call x1, Pallas kernels, attention(): pl.pallas_call(attention_kernel, grid=(count // LEN, HEADS), in_specs=in_...  22.8 us
    ppermute x5, waiting for transfers between devices, total_small(): value = value + lax.ppermute(value, axis, neighbours(axis, mask))  22.1 us
    ppermute x12, waiting for transfers between devices, swap(): return lax.ppermute(part, GROUP, perm)  21.8 us
  transfers between devices with their start and end apart: 30, of which 12 were waited for; matrix products, arithmetic and copies ran while one was open for 13% of the time, Pallas kernels for 5%

profile of v2, /device:TPU:0, one launch (start us, length us, event | category | flops | bytes accessed | tf_op | source)
XLA Modules:
  0.0 449.1 jit_solution(4481131965033719727)
XLA Ops:
  9.5 2.6 pad_maximum_fusion.4
  13.2 2.5 collective-permute-start.2
  21.4 3.0 multiply_sine_fusion
  24.5 39.4 %all-gather.2 = f32[4,160,4]{1,2,0:T(4,128)S(1)} all-gather(f32[1,160,4]{1,2,0:T(4,128)S(1)} %maximum_bitcast_fusion), channel_id=1, replica_groups=mesh['dp'=8,'row'=2,'col'=2] {'row','col'}, dimensions={0}, use_global_device_ids=true | all-gather | bytes 12800 | tf_op jit(solution)/shard_map/all_gather | solution.py:496
  78.6 22.8 %shard_map.280 = (f32[1024,1024]{1,0:T(8,128)}, f32[1024,256]{1,0:T(8,128)}, bf16[1024,1024]{1,0:T(8,128)(2,1)}, bf16[1024,256]{1,0:T(8,128)(2,1)}, bf16[1024,25...) custom-call(bf16[1024,640]{1,0:T(8,128)(2,1)} %pad_maximum_fusion.6.x_ref, ...), custom_call_target="tpu_custom_call" | custom-call | flops 5771362304 | bytes 16777216 | tf_op jit(solution)/shard_map/pallas_call | solution.py:320
  101.4 15.4 %all-gather.8.cloned.1.call-done = bf16[1280,3072]{1,0:T(8,128)(2,1)} async-done(((bf16[320,3072]{1,0:T(8,128)(2,1)}), bf16[1280,3072]{1,0:T(8,128)(2,1)}) %all-gather.8.cloned.1.call-update) | async-done | bytes 7864336 | tf_op jit(solution)/shard_map/all_gather | solution.py:60
  116.8 42.9 %shard_map.281 = (bf16[1024,640]{1,0:T(8,128)(2,1)}, f32[1024,640]{1,0:T(8,128)}, f32[1,640]{1,0:T(1,128)}, f32[1,640]{1,0:T(1,128)}, bf16[2,2,320,1024]{3,2,1,0...) custom-call(f32[1024,640]{1,0:T(8,128)} %get-tuple-element.39.middle_ref, ...), custom_call_target="tpu_custom_call" | custom-call | flops 24159191040 | bytes 47185920 | tf_op jit(solution)/shard_map/pallas_call | solution.py:445
  159.7 32.2 %shard_map.282 = (bf16[2,2,320,512]{3,2,1,0:T(8,128)(2,1)}, bf16[2,2,320,128]{3,2,1,0:T(8,128)(2,1)}, bf16[2,2,320,128]{3,2,1,0:T(8,128)(2,1)}, bf16[2,2,320,512...) custom-call(bf16[1024,640]{1,0:T(8,128)(2,1)} %pad_maximum_fusion.6., ...), custom_call_target="tpu_custom_call" | custom-call | flops 12750684160 | bytes 20480000 | tf_op jit(solution)/shard_map/pallas_call | solution.py:340
  195.6 4.3 pad_maximum_fusion
  208.2 2.9 collective-permute-done.22
  211.4 16.9 %collective-permute-done.23 = f32[3072]{0:T(1024)S(1)} collective-permute-done((f32[3072]{0:T(1024)S(1)}, f32[3072]{0:T(1024)S(1)}, u32[]{:S(2)}, u32[]{:S(2)}) %collective-permute-start.23) | collective-permute-done | bytes 12320 | tf_op jit(solution)/shard_map/ppermute | solution.py:106
  236.3 2.4 collective-permute-start.26
  245.0 7.2 %collective-permute-done.14 = bf16[160,1280]{1,0:T(8,128)(2,1)S(1)} collective-permute-done((bf16[160,1280]{1,0:T(8,128)(2,1)}, bf16[160,1280]{1,0:T(8,128)(2,1)S(1)}, u32[]{:S(2)}, u32[]{:S(2)}) %collective-permute-start.14) | collective-permute-done | bytes 409632 | tf_op jit(solution)/shard_map/ppermute | solution.py:76
  256.0 3.6 collective-permute-done.10
  263.8 8.7 %collective-permute-done.8 = bf16[1024,160]{1,0:T(8,128)(2,1)S(1)} collective-permute-done((bf16[1024,160]{1,0:T(8,128)(2,1)}, bf16[1024,160]{1,0:T(8,128)(2,1)S(1)}, u32[]{:S(2)}, u32[]{:S(2)}) %collective-permute-start.8) | collective-permute-done | bytes 327712 | tf_op jit(solution)/shard_map/ppermute | solution.py:124
  272.6 9.5 %collective-permute-done.7 = bf16[1024,160]{1,0:T(8,128)(2,1)S(1)} collective-permute-done((bf16[1024,160]{1,0:T(8,128)(2,1)S(1)}, bf16[1024,160]{1,0:T(8,128)(2,1)S(1)}, u32[]{:S(2)}, u32[]{:S(2)}) %collective-permute-start.7) | collective-permute-done | bytes 327712 | tf_op jit(solution)/shard_map/ppermute | solution.py:124
  282.7 4.9 %add_convert_fusion = bf16[1,2,320,3072]{3,2,0,1:T(8,128)(2,1)S(1)} fusion(bf16[1,2,320,3072]{3,2,0,1:T(8,128)(2,1)} %collective-permute-done.20, bf16[2,2,320,3072]{3,2,0,1:T(8,128)(2,1)} %copy-done, s32[]{:T(128)S(6)} %select_n.199), kind=kLoop, calls=%fused_computation.1 | loop fusion | flops 7864320 | bytes 11796484 | tf_op jit(solution)/shard_map/convert_element_type | solution.py:77
  289.2 2.3 collective-permute-start.21
  292.2 2.4 collective-permute-start.16
  304.6 3.9 collective-permute-done.17
  308.7 26.3 %collective-permute-done.21 = bf16[1,320,3072]{2,1,0:T(8,128)(2,1)} collective-permute-done((bf16[1,320,3072]{2,1,0:T(8,128)(2,1)}, bf16[1,320,3072]{2,1,0:T(8,128)(2,1)}, u32[]{:S(2)}, u32[]{:S(2)}) %collective-permute-start.21) | collective-permute-done | bytes 1966112 | tf_op jit(solution)/shard_map/ppermute | solution.py:76
  335.0 4.2 fusion.1
  342.0 13.2 %collective-permute-done.19 = bf16[160,1280]{1,0:T(8,128)(2,1)S(1)} collective-permute-done((bf16[160,1280]{1,0:T(8,128)(2,1)S(1)}, bf16[160,1280]{1,0:T(8,128)(2,1)S(1)}, u32[]{:S(2)}, u32[]{:S(2)}) %collective-permute-start.19) | collective-permute-done | bytes 409632 | tf_op jit(solution)/shard_map/ppermute | solution.py:82
  358.0 79.9 %all-reduce.2.cloned.1.call-done = bf16[320,3072]{1,0:T(8,128)(2,1)} async-done(((bf16[320,3072]{1,0:T(8,128)(2,1)}), bf16[320,3072]{1,0:T(8,128)(2,1)}) %all-reduce.2.cloned.1.call-update) | async-done | bytes 1966096 | tf_op jit(solution)/shard_map/psum | solution.py:521
  (176 shorter events, 81.0 us)
Async XLA Ops:
  7.2 71.4 %all-gather.6.cloned.1.call-start = ((), (), s32[]{:S(2)}) async-start(), calls=%async_computation.1 | async-start | bytes 4096000 | tf_op jit(solution)/shard_map/all_gather | solution.py:60
  9.5 107.3 %all-gather.8.cloned.1.call-start = ((), (), s32[]{:S(2)}) async-start(), calls=%async_computation.2 | async-start | bytes 9830400 | tf_op jit(solution)/shard_map/all_gather | solution.py:60
  12.2 425.8 %all-reduce.2.cloned.1.call-start = ((), (), s32[]{:S(2)}) async-start(), calls=%async_computation | async-start | bytes 3932160 | tf_op jit(solution)/shard_map/psum | solution.py:521
  13.2 50.7 %collective-permute-start.2 = (bf16[1024,160]{0,1:T(8,128)(2,1)}, bf16[1024,160]{0,1:T(8,128)(2,1)S(1)}, u32[]{:S(2)}, u32[]{:S(2)}) collective-permute-start(bf16[1024,160]{0,1:T(8,128)(2,1)} %get-tuple-element.95), channel_id=1, source_target_pairs={{0,3},{1,2},{2,1},{3,0},{4,7},{5,6},{6,5},{7,4},{8,11},{9,10},{10,... | collective-permute-start | bytes 983048 | tf_op jit(solution)/shard_map/ppermute | solution.py:124
  15.7 50.9 %collective-permute-start.1 = (bf16[1024,160]{0,1:T(8,128)(2,1)}, bf16[1024,160]{0,1:T(8,128)(2,1)S(1)}, u32[]{:S(2)}, u32[]{:S(2)}) collective-permute-start(bf16[1024,160]{0,1:T(8,128)(2,1)} %get-tuple-element.96), channel_id=1, source_target_pairs={{0,2},{1,3},{2,0},{3,1},{4,6},{5,7},{6,4},{7,5},{8,10},{9,11},{10,... | collective-permute-start | bytes 983048 | tf_op jit(solution)/shard_map/ppermute | solution.py:124
  16.3 50.3 %collective-permute-start = (bf16[1024,160]{0,1:T(8,128)(2,1)S(1)}, bf16[1024,160]{0,1:T(8,128)(2,1)S(1)}, u32[]{:S(2)}, u32[]{:S(2)}) collective-permute-start(bf16[1024,160]{0,1:T(8,128)(2,1)S(1)} %get-tuple-element.94), channel_id=1, source_target_pairs={{0,1},{1,0},{2,3},{3,2},{4,5},{5,4},{6,7},{7,6},{8,9},{9,8},{10,11... | collective-permute-start | bytes 983048 | tf_op jit(solution)/shard_map/ppermute | solution.py:124
  18.6 49.2 %collective-permute-start.5 = (bf16[1024,160]{0,1:T(8,128)(2,1)}, bf16[1024,160]{0,1:T(8,128)(2,1)S(1)}, u32[]{:S(2)}, u32[]{:S(2)}) collective-permute-start(bf16[1024,160]{0,1:T(8,128)(2,1)} %get-tuple-element.87), channel_id=1, source_target_pairs={{0,3},{1,2},{2,1},{3,0},{4,7},{5,6},{6,5},{7,4},{8,11},{9,10},{10,... | collective-permute-start | bytes 983048 | tf_op jit(solution)/shard_map/ppermute | solution.py:124
  20.0 47.7 %collective-permute-start.4 = (bf16[1024,160]{0,1:T(8,128)(2,1)}, bf16[1024,160]{0,1:T(8,128)(2,1)}, u32[]{:S(2)}, u32[]{:S(2)}) collective-permute-start(bf16[1024,160]{0,1:T(8,128)(2,1)} %get-tuple-element.88), channel_id=1, source_target_pairs={{0,2},{1,3},{2,0},{3,1},{4,6},{5,7},{6,4},{7,5},{8,10},{9,11},{10,... | collective-permute-start | bytes 983048 | tf_op jit(solution)/shard_map/ppermute | solution.py:124
  195.3 9.2 %collective-permute-start.12 = (bf16[1,2,320,1280]{3,2,0,1:T(8,128)(2,1)}, bf16[1,2,320,1280]{3,2,0,1:T(8,128)(2,1)}, u32[]{:S(2)}, u32[]{:S(2)}) collective-permute-start(bf16[1,2,320,1280]{3,2,0,1:T(8,128)(2,1)} %constant_dynamic-slice_fusion.4), channel_id=1, source_target_pairs={{0,1},{1,0},{2,3},{3,2},{4,5},{5,4},{6,7},{7,6},{8,9},{9,8},{10,11... | collective-permute-start | bytes 4915208 | tf_op jit(solution)/shard_map/ppermute | solution.py:76
  204.2 78.5 %collective-permute-start.20 = (bf16[1,2,320,3072]{3,2,0,1:T(8,128)(2,1)}, bf16[1,2,320,3072]{3,2,0,1:T(8,128)(2,1)}, u32[]{:S(2)}, u32[]{:S(2)}) collective-permute-start(bf16[1,2,320,3072]{3,2,0,1:T(8,128)(2,1)} %constant_dynamic-slice_fusion.1), channel_id=1, source_target_pairs={{0,1},{1,0},{2,3},{3,2},{4,5},{5,4},{6,7},{7,6},{8,9},{9,8},{10,11... | collective-permute-start | bytes 11796488 | tf_op jit(solution)/shard_map/ppermute | solution.py:76
  207.6 31.1 %collective-permute-start.13 = (bf16[1,320,1280]{2,1,0:T(8,128)(2,1)S(1)}, bf16[1,320,1280]{2,1,0:T(8,128)(2,1)S(1)}, u32[]{:S(2)}, u32[]{:S(2)}) collective-permute-start(bf16[1,320,1280]{2,1,0:T(8,128)(2,1)S(1)} %dynamic-slice_bitcast_fusion.1), channel_id=1, source_target_pairs={{0,2},{2,0},{1,3},{3,1},{4,6},{6,4},{5,7},{7,5},{8,10},{10,8},{9,1... | collective-permute-start | bytes 2457608 | tf_op jit(solution)/shard_map/ppermute | solution.py:76
  211.1 17.3 %collective-permute-start.23 = (f32[3072]{0:T(1024)S(1)}, f32[3072]{0:T(1024)S(1)}, u32[]{:S(2)}, u32[]{:S(2)}) collective-permute-start(f32[3072]{0:T(1024)S(1)} %add.202), channel_id=1, source_target_pairs={{0,2},{2,0},{1,3},{3,1},{4,6},{6,4},{5,7},{7,5},{8,10},{10,8},{9,1... | collective-permute-start | bytes 36872 | tf_op jit(solution)/shard_map/ppermute | solution.py:106
  235.7 18.4 %collective-permute-start.11 = (bf16[1024,160]{1,0:T(8,128)(2,1)}, bf16[1024,160]{1,0:T(8,128)(2,1)}, u32[]{:S(2)}, u32[]{:S(2)}) collective-permute-start(bf16[1024,160]{1,0:T(8,128)(2,1)} %get-tuple-element.74), channel_id=1, source_target_pairs={{0,3},{1,2},{2,1},{3,0},{4,7},{5,6},{6,5},{7,4},{8,11},{9,10},{10,... | collective-permute-start | bytes 983048 | tf_op jit(solution)/shard_map/ppermute | solution.py:124
  235.7 24.0 %collective-permute-start.10 = (bf16[1024,160]{1,0:T(8,128)(2,1)}, bf16[1024,160]{1,0:T(8,128)(2,1)}, u32[]{:S(2)}, u32[]{:S(2)}) collective-permute-start(bf16[1024,160]{1,0:T(8,128)(2,1)} %get-tuple-element.75), channel_id=1, source_target_pairs={{0,2},{1,3},{2,0},{3,1},{4,6},{5,7},{6,4},{7,5},{8,10},{9,11},{10,... | collective-permute-start | bytes 983048 | tf_op jit(solution)/shard_map/ppermute | solution.py:124
  239.7 12.5 %collective-permute-start.14 = (bf16[160,1280]{1,0:T(8,128)(2,1)}, bf16[160,1280]{1,0:T(8,128)(2,1)S(1)}, u32[]{:S(2)}, u32[]{:S(2)}) collective-permute-start(bf16[160,1280]{1,0:T(8,128)(2,1)} %dynamic-slice_bitcast_fusion.4), channel_id=1, source_target_pairs={{0,4},{4,0},{8,12},{12,8},{16,20},{20,16},{24,28},{28,24},{1,5},{5... | collective-permute-start | bytes 1228808 | tf_op jit(solution)/shard_map/ppermute | solution.py:76
  243.0 18.3 %collective-permute-start.9 = (bf16[1024,160]{1,0:T(8,128)(2,1)}, bf16[1024,160]{1,0:T(8,128)(2,1)}, u32[]{:S(2)}, u32[]{:S(2)}) collective-permute-start(bf16[1024,160]{1,0:T(8,128)(2,1)} %get-tuple-element.76), channel_id=1, source_target_pairs={{0,1},{1,0},{2,3},{3,2},{4,5},{5,4},{6,7},{7,6},{8,9},{9,8},{10,11... | collective-permute-start | bytes 983048 | tf_op jit(solution)/shard_map/ppermute | solution.py:124
  253.0 19.6 %collective-permute-start.8 = (bf16[1024,160]{1,0:T(8,128)(2,1)}, bf16[1024,160]{1,0:T(8,128)(2,1)S(1)}, u32[]{:S(2)}, u32[]{:S(2)}) collective-permute-start(bf16[1024,160]{1,0:T(8,128)(2,1)} %get-tuple-element.78), channel_id=1, source_target_pairs={{0,3},{1,2},{2,1},{3,0},{4,7},{5,6},{6,5},{7,4},{8,11},{9,10},{10,... | collective-permute-start | bytes 983048 | tf_op jit(solution)/shard_map/ppermute | solution.py:124
  254.1 28.0 %collective-permute-start.7 = (bf16[1024,160]{1,0:T(8,128)(2,1)S(1)}, bf16[1024,160]{1,0:T(8,128)(2,1)S(1)}, u32[]{:S(2)}, u32[]{:S(2)}) collective-permute-start(bf16[1024,160]{1,0:T(8,128)(2,1)S(1)} %get-tuple-element.79), channel_id=1, source_target_pairs={{0,2},{1,3},{2,0},{3,1},{4,6},{5,7},{6,4},{7,5},{8,10},{9,11},{10,... | collective-permute-start | bytes 983048 | tf_op jit(solution)/shard_map/ppermute | solution.py:124
  259.7 22.4 %collective-permute-start.6 = (bf16[1024,160]{1,0:T(8,128)(2,1)S(1)}, bf16[1024,160]{1,0:T(8,128)(2,1)S(1)}, u32[]{:S(2)}, u32[]{:S(2)}) collective-permute-start(bf16[1024,160]{1,0:T(8,128)(2,1)S(1)} %get-tuple-element.80), channel_id=1, source_target_pairs={{0,1},{1,0},{2,3},{3,2},{4,5},{5,4},{6,7},{7,6},{8,9},{9,8},{10,11... | collective-permute-start | bytes 983048 | tf_op jit(solution)/shard_map/ppermute | solution.py:124
  261.3 21.3 %collective-permute-start.15 = (bf16[80,1280]{1,0:T(8,128)(2,1)S(1)}, bf16[80,1280]{1,0:T(8,128)(2,1)S(1)}, u32[]{:S(2)}, u32[]{:S(2)}) collective-permute-start(bf16[80,1280]{1,0:T(8,128)(2,1)S(1)} %constant_dynamic-slice_fusion.3), channel_id=1, source_target_pairs={{0,8},{4,12},{8,0},{12,4},{16,24},{20,28},{24,16},{28,20},{1,9},{5... | collective-permute-start | bytes 614408 | tf_op jit(solution)/shard_map/ppermute | solution.py:76
  289.2 45.8 %collective-permute-start.21 = (bf16[1,320,3072]{2,1,0:T(8,128)(2,1)}, bf16[1,320,3072]{2,1,0:T(8,128)(2,1)}, u32[]{:S(2)}, u32[]{:S(2)}) collective-permute-start(bf16[1,320,3072]{2,1,0:T(8,128)(2,1)} %dynamic-slice_bitcast_fusion), channel_id=1, source_target_pairs={{0,2},{2,0},{1,3},{3,1},{4,6},{6,4},{5,7},{7,5},{8,10},{10,8},{9,1... | collective-permute-start | bytes 5898248 | tf_op jit(solution)/shard_map/ppermute | solution.py:76
  292.2 7.9 %collective-permute-start.16 = (bf16[40,1280]{1,0:T(8,128)(2,1)}, bf16[40,1280]{1,0:T(8,128)(2,1)}, u32[]{:S(2)}, u32[]{:S(2)}) collective-permute-start(bf16[40,1280]{1,0:T(8,128)(2,1)} %constant_dynamic-slice_fusion.2), channel_id=1, source_target_pairs={{0,16},{4,20},{8,24},{12,28},{16,0},{20,4},{24,8},{28,12},{1,17},{... | collective-permute-start | bytes 307208 | tf_op jit(solution)/shard_map/ppermute | solution.py:76
  308.6 30.6 %collective-permute-start.18 = (bf16[80,1280]{1,0:T(8,128)(2,1)S(1)}, bf16[80,1280]{1,0:T(8,128)(2,1)S(1)}, u32[]{:S(2)}, u32[]{:S(2)}) collective-permute-start(bf16[80,1280]{1,0:T(8,128)(2,1)S(1)} %pad_maximum_fusion.13), channel_id=1, source_target_pairs={{0,8},{4,12},{8,0},{12,4},{16,24},{20,28},{24,16},{28,20},{1,9},{5... | collective-permute-start | bytes 614408 | tf_op jit(solution)/shard_map/ppermute | solution.py:82
  339.3 15.9 %collective-permute-start.19 = (bf16[160,1280]{1,0:T(8,128)(2,1)S(1)}, bf16[160,1280]{1,0:T(8,128)(2,1)S(1)}, u32[]{:S(2)}, u32[]{:S(2)}) collective-permute-start(bf16[160,1280]{1,0:T(8,128)(2,1)S(1)} %pad_maximum_fusion.12), channel_id=1, source_target_pairs={{0,4},{4,0},{8,12},{12,8},{16,20},{20,16},{24,28},{28,24},{1,5},{5... | collective-permute-start | bytes 1228808 | tf_op jit(solution)/shard_map/ppermute | solution.py:82
  (31 other events, 171.7 us)
Sparse Core Ops, SparseCore 0:
  10.2 49.6 all-gather.5
  61.4 55.2 all-gather.7
  339.3 98.5 all-reduce.1
